TPU v7x, 256 devices: a whole 4x4x8 slice. The times are simulated.
256 devices in a mesh: seq: 16 (over x, y), head: 16 (over z, core).
Axes of the slice: x: 4, y: 4, z: 8, core: 2. Of those that a mesh axis runs over, the one named last changes fastest.
Arguments:
- activations: bfloat16 [65536, 768], P(('seq', 'head')), may hold values from -6 to 6
- ln_gain: bfloat16 [768], replicated, may hold values from 0.099609375 to 1.8984375
- w_query: bfloat16 [768, 768], replicated
- w_key: bfloat16 [768, 768], replicated
- w_value: bfloat16 [768, 768], replicated, may hold values from -0.21875 to 0.21875
- w_gate: bfloat16 [768, 768], replicated, may hold values from -0.21875 to 0.21875
- w_out: bfloat16 [768, 768], replicated, may hold values from -0.21875 to 0.21875
- bias_tiles: bfloat16 [16, 16, 128, 256], P(None, 'head'), may hold values from -6 to 6
- crop_lengths: int32 [16], replicated, may hold values from 1 to 16384, 65536 in all
- tile_index: int32 [512], P('seq'), may hold values from 0 to 15
- d_out: bfloat16 [65536, 768], P(('seq', 'head')), may hold values from -6 to 6
Outputs:
- d_activations: bfloat16 [65536, 768], P(('seq', 'head'))
- d_bias: float32 [16, 16, 128, 256], P(None, 'head')
Inputs may be any that keep to these rules, and one draw needn't show every extreme that they name: crop_lengths sum to 65536; the longest crop is exactly 16384 rows.
All inputs are finite; a program needn't handle non-finite values.
Results may differ from a plain program's by a relative error of at most 0.039.
The roundings to bfloat16 on the way count: a program that leaves them out, or rounds other values in their place, can miss the bound.
Values may be sent and summed in bfloat16 or wider, within the bound.
A program may use at most 128 MiB of HBM per device.

v0:
```python
import math

import jax
import jax.numpy as jnp
from jax import lax
from jax.sharding import PartitionSpec as P

BLOCK = 128


eps = 1e-05


def passed_along(array, axis, by):
    length = lax.axis_size(axis)
    pairs = [(i, i + by) for i in range(length) if 0 <= i + by < length]
    return lax.ppermute(array, axis, pairs)


def norm_rows(activations, ln_gain):
    values = activations.astype(jnp.float32)
    centred = values - jnp.mean(values, axis=1, keepdims=True)
    inverse = lax.rsqrt(jnp.mean(centred * centred, axis=1, keepdims=True) + eps)
    scaled = centred * inverse
    normed = (scaled * ln_gain.astype(jnp.float32)[None, :]).astype(jnp.bfloat16)
    return (normed, scaled, inverse)


def norm_back(d_normed, scaled, inverse, ln_gain):
    d_scaled = d_normed * ln_gain.astype(jnp.float32)[None, :]
    centre = jnp.mean(d_scaled, axis=1, keepdims=True)
    along = jnp.mean(d_scaled * scaled, axis=1, keepdims=True)
    return (inverse * (d_scaled - centre - scaled * along)).astype(jnp.bfloat16)


def window_mask(first, blocks, crop_lengths):
    bounds = jnp.cumsum(crop_lengths)

    def crop_of(positions):
        return jnp.sum((bounds[None, :] <= positions[:, None]).astype(jnp.int32), axis=1)

    queries = first + jnp.arange(blocks * BLOCK, dtype=jnp.int32)
    starts = first + BLOCK * jnp.arange(blocks, dtype=jnp.int32) - BLOCK
    key_pos = starts[:, None] + jnp.arange(2 * BLOCK, dtype=jnp.int32)[None, :]
    query_crop = crop_of(queries).reshape(blocks, BLOCK)
    key_crop = crop_of(key_pos.reshape(-1)).reshape(blocks, 2 * BLOCK)
    return (key_pos >= 0)[:, None, :] & (query_crop[:, :, None] == key_crop[:, None, :])


def attention_pass(
    queries, keys, values, keys_before, values_before, grad_out, bias, allowed, heads_here
):
    rows, width = queries.shape
    blocks = rows // BLOCK
    size = width // heads_here
    scale = 1.0 / math.sqrt(size)

    def split(array):
        return array.reshape(blocks, BLOCK, heads_here, size)

    query_blocks = split(queries)
    key_blocks = split(keys)
    value_blocks = split(values)
    grad_blocks = split(grad_out)
    key_prev = jnp.concatenate(
        [keys_before.reshape(1, BLOCK, heads_here, size), key_blocks[:-1]], axis=0
    )
    value_prev = jnp.concatenate(
        [values_before.reshape(1, BLOCK, heads_here, size), value_blocks[:-1]], axis=0
    )
    key_window = jnp.concatenate([key_prev, key_blocks], axis=1)
    value_window = jnp.concatenate([value_prev, value_blocks], axis=1)
    mask = allowed[:, None, :, :]
    scores = (
        jnp.einsum("nihd,njhd->nhij", query_blocks, key_window, preferred_element_type=jnp.float32)
        * scale
        + bias
    )
    scores = jnp.where(mask, scores, -1e30)
    top = jnp.max(scores, axis=3, keepdims=True)
    weights = jnp.where(mask, jnp.exp(scores - top), 0.0)
    probs = weights / jnp.sum(weights, axis=3, keepdims=True)
    probs_low = probs.astype(jnp.bfloat16)
    attended = jnp.einsum(
        "nhij,njhd->nihd", probs_low, value_window, preferred_element_type=jnp.float32
    )
    attended = attended.astype(jnp.bfloat16).reshape(rows, width)
    d_probs = jnp.einsum(
        "nihd,njhd->nhij", grad_blocks, value_window, preferred_element_type=jnp.float32
    )
    d_scores = probs * (d_probs - jnp.sum(probs * d_probs, axis=3, keepdims=True))
    d_low = d_scores.astype(jnp.bfloat16)
    d_queries = (
        jnp.einsum("nhij,njhd->nihd", d_low, key_window, preferred_element_type=jnp.float32) * scale
    )
    d_queries = d_queries.astype(jnp.bfloat16).reshape(rows, width)
    d_key_window = (
        jnp.einsum("nhij,nihd->njhd", d_low, query_blocks, preferred_element_type=jnp.float32)
        * scale
    )
    d_value_window = jnp.einsum(
        "nhij,nihd->njhd", probs_low, grad_blocks, preferred_element_type=jnp.float32
    )
    empty = jnp.zeros((1, BLOCK, heads_here, size), jnp.float32)
    d_keys = d_key_window[:, BLOCK:] + jnp.concatenate([d_key_window[1:, :BLOCK], empty], axis=0)
    d_values = d_value_window[:, BLOCK:] + jnp.concatenate(
        [d_value_window[1:, :BLOCK], empty], axis=0
    )
    return (
        attended,
        d_queries,
        d_keys.reshape(rows, width),
        d_values.reshape(rows, width),
        d_key_window[0, :BLOCK].reshape(BLOCK, width),
        d_value_window[0, :BLOCK].reshape(BLOCK, width),
        d_scores,
    )


def back_product(gradient, weight):
    return lax.dot_general(
        gradient, weight, (((1,), (1,)), ((), ())), preferred_element_type=jnp.float32
    )


def shards(
    activations,
    ln_gain,
    w_query,
    w_key,
    w_value,
    w_gate,
    w_out,
    bias_tiles,
    crop_lengths,
    tile_index,
    d_out,
):
    heads_here = bias_tiles.shape[1]
    normed, scaled, inverse = norm_rows(activations, ln_gain)
    queries = jnp.dot(normed, w_query, preferred_element_type=jnp.float32).astype(jnp.bfloat16)
    keys = jnp.dot(normed, w_key, preferred_element_type=jnp.float32).astype(jnp.bfloat16)
    values = jnp.dot(normed, w_value, preferred_element_type=jnp.float32).astype(jnp.bfloat16)
    gate_input = jnp.dot(normed, w_gate, preferred_element_type=jnp.float32).astype(jnp.bfloat16)
    d_mixed = back_product(d_out, w_out).astype(jnp.bfloat16)
    head_q, head_k, head_v, head_gin, head_dmix = (
        lax.all_to_all(queries, "head", split_axis=1, concat_axis=0, tiled=True),
        lax.all_to_all(keys, "head", split_axis=1, concat_axis=0, tiled=True),
        lax.all_to_all(values, "head", split_axis=1, concat_axis=0, tiled=True),
        lax.all_to_all(gate_input, "head", split_axis=1, concat_axis=0, tiled=True),
        lax.all_to_all(d_mixed, "head", split_axis=1, concat_axis=0, tiled=True),
    )
    head_gate = jax.nn.sigmoid(head_gin.astype(jnp.float32))
    head_grad = (head_dmix.astype(jnp.float32) * head_gate).astype(jnp.bfloat16)
    group_rows = head_q.shape[0]
    blocks = group_rows // BLOCK
    first = lax.axis_index("seq") * group_rows
    allowed = window_mask(first, blocks, crop_lengths)
    picks = (
        tile_index[:, None] == jnp.arange(bias_tiles.shape[0], dtype=jnp.int32)[None, :]
    ).astype(jnp.bfloat16)
    bias = jnp.einsum("nt,thij->nhij", picks, bias_tiles, preferred_element_type=jnp.float32)
    keys_before, values_before = passed_along((head_k[-BLOCK:], head_v[-BLOCK:]), "seq", 1)
    attended, d_queries, d_keys, d_values, d_key_edge, d_value_edge, d_scores = attention_pass(
        head_q, head_k, head_v, keys_before, values_before, head_grad, bias, allowed, heads_here
    )
    key_after, value_after = (
        passed_along(d_key_edge.astype(jnp.bfloat16), "seq", -1).astype(d_key_edge.dtype),
        passed_along(d_value_edge.astype(jnp.bfloat16), "seq", -1).astype(d_value_edge.dtype),
    )
    d_keys = jnp.concatenate([d_keys[:-BLOCK], d_keys[-BLOCK:] + key_after], axis=0).astype(
        jnp.bfloat16
    )
    d_values = jnp.concatenate([d_values[:-BLOCK], d_values[-BLOCK:] + value_after], axis=0).astype(
        jnp.bfloat16
    )
    local_tiles = jnp.einsum(
        "nt,nhij->thij", picks.astype(jnp.float32), d_scores, precision=lax.Precision.HIGHEST
    )
    d_bias = lax.psum(local_tiles.astype(jnp.bfloat16), "seq").astype(jnp.float32)
    head_dgate = (
        head_dmix.astype(jnp.float32) * attended.astype(jnp.float32) * head_gate * (1.0 - head_gate)
    ).astype(jnp.bfloat16)
    row_dq, row_dk, row_dv, d_gate = (
        lax.all_to_all(d_queries, "head", split_axis=0, concat_axis=1, tiled=True),
        lax.all_to_all(d_keys, "head", split_axis=0, concat_axis=1, tiled=True),
        lax.all_to_all(d_values, "head", split_axis=0, concat_axis=1, tiled=True),
        lax.all_to_all(head_dgate, "head", split_axis=0, concat_axis=1, tiled=True),
    )
    d_normed = back_product(row_dq, w_query)
    d_normed = d_normed + back_product(row_dk, w_key)
    d_normed = d_normed + back_product(row_dv, w_value)
    d_normed = d_normed + back_product(d_gate, w_gate)
    d_activations = norm_back(d_normed, scaled, inverse, ln_gain)
    return (d_activations, d_bias)


def solution(mesh):
    return jax.shard_map(
        shards,
        mesh=mesh,
        in_specs=(
            P(("seq", "head"), None),
            P(),
            P(),
            P(),
            P(),
            P(),
            P(),
            P(None, "head", None, None),
            P(),
            P("seq"),
            P(("seq", "head"), None),
        ),
        out_specs=(P(("seq", "head"), None), P(None, "head", None, None)),
        check_vma=False,
    )
```

profile of v0, /device:TPU:8, one launch (start us, length us, event | category | flops | bytes accessed | tf_op | source)
XLA Modules:
  0.0 312.2 jit_solution(1983866665688578780)
XLA Ops:
  10.4 1.9 convolution_convert_fusion.4
  13.3 8.6 %all-to-all-start.1 = ((bf16[256,16,48]{0,2,1:T(8,128)(2,1)}), bf16[256,16,48]{0,2,1:T(8,128)(2,1)S(1)}, u32[]{:S(2)}, u32[]{:S(2)}) async-start(bf16[256,16,48]{0,2,1:T(8,128)(2,1)} %bitcast.6), calls=%async_computation.1 | async-start | bytes 786432 | tf_op jit(solution)/shard_map/all_to_all | solution.py:147
  23.3 12.2 %all-to-all-done.1 = bf16[256,16,48]{0,2,1:T(8,128)(2,1)S(1)} async-done(((bf16[256,16,48]{0,2,1:T(8,128)(2,1)}), bf16[256,16,48]{0,2,1:T(8,128)(2,1)S(1)}, u32[]{:S(2)}, u32[]{:S(2)}) %all-to-all-start.1) | async-done | bytes 393248 | tf_op jit(solution)/shard_map/all_to_all | solution.py:147
  35.5 3.7 %all-to-all-start.3 = ((bf16[256,16,48]{0,2,1:T(8,128)(2,1)}), bf16[256,16,48]{0,2,1:T(8,128)(2,1)S(1)}, u32[]{:S(2)}, u32[]{:S(2)}) async-start(bf16[256,16,48]{0,2,1:T(8,128)(2,1)} %bitcast.11), calls=%async_computation.3 | async-start | bytes 786432 | tf_op jit(solution)/shard_map/all_to_all | solution.py:150
  40.6 1.9 copy.112
  42.5 10.6 %all-to-all-done.3 = bf16[256,16,48]{0,2,1:T(8,128)(2,1)S(1)} async-done(((bf16[256,16,48]{0,2,1:T(8,128)(2,1)}), bf16[256,16,48]{0,2,1:T(8,128)(2,1)S(1)}, u32[]{:S(2)}, u32[]{:S(2)}) %all-to-all-start.3) | async-done | bytes 393248 | tf_op jit(solution)/shard_map/all_to_all | solution.py:150
  53.0 3.6 %all-to-all-start.4 = ((bf16[256,16,48]{0,2,1:T(8,128)(2,1)}), bf16[256,16,48]{0,2,1:T(8,128)(2,1)S(1)}, u32[]{:S(2)}, u32[]{:S(2)}) async-start(bf16[256,16,48]{0,2,1:T(8,128)(2,1)} %bitcast.13), calls=%async_computation.4 | async-start | bytes 786432 | tf_op jit(solution)/shard_map/all_to_all | solution.py:149
  59.4 11.0 %all-to-all-done.4 = bf16[256,16,48]{0,2,1:T(8,128)(2,1)S(1)} async-done(((bf16[256,16,48]{0,2,1:T(8,128)(2,1)}), bf16[256,16,48]{0,2,1:T(8,128)(2,1)S(1)}, u32[]{:S(2)}, u32[]{:S(2)}) %all-to-all-start.4) | async-done | bytes 393248 | tf_op jit(solution)/shard_map/all_to_all | solution.py:149
  70.4 3.7 %all-to-all-start = ((bf16[256,16,48]{0,2,1:T(8,128)(2,1)}), bf16[256,16,48]{0,2,1:T(8,128)(2,1)S(1)}, u32[]{:S(2)}, u32[]{:S(2)}) async-start(bf16[256,16,48]{0,2,1:T(8,128)(2,1)} %bitcast), calls=%async_computation | async-start | bytes 786432 | tf_op jit(solution)/shard_map/all_to_all | solution.py:148
  79.9 8.0 %all-to-all-done = bf16[256,16,48]{0,2,1:T(8,128)(2,1)S(1)} async-done(((bf16[256,16,48]{0,2,1:T(8,128)(2,1)}), bf16[256,16,48]{0,2,1:T(8,128)(2,1)S(1)}, u32[]{:S(2)}, u32[]{:S(2)}) %all-to-all-start) | async-done | bytes 393248 | tf_op jit(solution)/shard_map/all_to_all | solution.py:148
  87.9 3.7 %all-to-all-start.2 = ((bf16[256,16,48]{0,2,1:T(8,128)(2,1)}), bf16[256,16,48]{0,2,1:T(8,128)(2,1)S(1)}, u32[]{:S(2)}, u32[]{:S(2)}) async-start(bf16[256,16,48]{0,2,1:T(8,128)(2,1)} %bitcast.168), calls=%async_computation.2 | async-start | bytes 786432 | tf_op jit(solution)/shard_map/all_to_all | solution.py:151
  95.5 4.1 %fusion.16 = f32[32,128,256]{2,0,1:T(8,128)} fusion(bf16[16,128,256]{2,1,0:T(8,128)(2,1)} %bitcast.180, s32[32]{0:T(128)} %param.20), kind=kOutput, calls=%fused_computation.29 | convolution fusion | flops 33554944 | bytes 5243008 | tf_op jit(solution)/shard_map/nt,thij->nhij/dot_general | solution.py:162
  107.0 3.5 %collective-permute-start.1 = (bf16[128,48]{0,1:T(8,128)(2,1)}, bf16[128,48]{0,1:T(8,128)(2,1)}, u32[]{:S(2)}, u32[]{:S(2)}) collective-permute-start(bf16[128,48]{0,1:T(8,128)(2,1)} %slice.78), channel_id=1, source_target_pairs={{0,16},{16,32},{32,48},{48,64},{64,80},{80,96},{96,112},{112,128},... | collective-permute-start | bytes 36872 | tf_op jit(solution)/shard_map/ppermute | solution.py:17
  110.5 3.4 %collective-permute-start = (bf16[128,48]{0,1:T(8,128)(2,1)S(1)}, bf16[128,48]{0,1:T(8,128)(2,1)}, u32[]{:S(2)}, u32[]{:S(2)}) collective-permute-start(bf16[128,48]{0,1:T(8,128)(2,1)S(1)} %slice.76), channel_id=1, source_target_pairs={{0,16},{16,32},{32,48},{48,64},{64,80},{80,96},{96,112},{112,128},... | collective-permute-start | bytes 36872 | tf_op jit(solution)/shard_map/ppermute | solution.py:17
  119.1 12.2 %fusion.67 = (f32[32,128]{1,0:T(8,128)S(1)}, f32[32,128,256]{2,1,0:T(8,128)}) fusion(s32[32,256]{1,0:T(8,128)} %eq.32, s32[32,128]{1,0:T(8,128)} %bitcast.184, pred[32,256]{1,0:T(8,128)(4,1)} %fusion.46, f32[32,128,256]{2,0,1:T(8,128)} %fusion.16, bf16[32,128,48]{1,0,2:T(8,128)(2,1)S(1)} %reshape.250, bf16[32,128,1,48]{1,3,0,2:T(8,128)(2,1)S(1)} %copy.101, ...), kind=kOutput, calls=%fused_computation.106 | convolution fusion | flops 113508608 | bytes 9641984 | tf_op jit(solution)/shard_map/sub | solution.py:81
  131.3 3.0 fusion.19
  134.9 2.6 multiply_reduce_fusion
  142.1 3.0 collective-permute-start.3
  147.0 1.9 all_to_all.125
  150.8 7.3 %all-to-all-start.5 = ((bf16[16,256,48]{1,2,0:T(8,128)(2,1)}), bf16[16,256,48]{1,2,0:T(8,128)(2,1)}, u32[]{:S(2)}, u32[]{:S(2)}) async-start(bf16[16,256,48]{1,2,0:T(8,128)(2,1)} %copy.119), calls=%async_computation.5 | async-start | bytes 786432 | tf_op jit(solution)/shard_map/all_to_all | solution.py:185
  160.1 1.9 collective-permute-start.2
  164.6 7.2 %all-to-all-done.5 = bf16[16,256,48]{1,2,0:T(8,128)(2,1)} async-done(((bf16[16,256,48]{1,2,0:T(8,128)(2,1)}), bf16[16,256,48]{1,2,0:T(8,128)(2,1)}, u32[]{:S(2)}, u32[]{:S(2)}) %all-to-all-start.5) | async-done | bytes 393248 | tf_op jit(solution)/shard_map/all_to_all | solution.py:185
  171.8 4.2 %all-to-all-start.7 = ((bf16[16,256,48]{1,2,0:T(8,128)(2,1)}), bf16[16,256,48]{1,2,0:T(8,128)(2,1)}, u32[]{:S(2)}, u32[]{:S(2)}) async-start(bf16[16,256,48]{1,2,0:T(8,128)(2,1)} %bitcast.169), calls=%async_computation.7 | async-start | bytes 786432 | tf_op jit(solution)/shard_map/all_to_all | solution.py:187
  179.1 10.6 %all-to-all-done.7 = bf16[16,256,48]{1,2,0:T(8,128)(2,1)} async-done(((bf16[16,256,48]{1,2,0:T(8,128)(2,1)}), bf16[16,256,48]{1,2,0:T(8,128)(2,1)}, u32[]{:S(2)}, u32[]{:S(2)}) %all-to-all-start.7) | async-done | bytes 393248 | tf_op jit(solution)/shard_map/all_to_all | solution.py:187
  189.7 4.2 %all-to-all-start.6 = ((bf16[16,256,48]{1,2,0:T(8,128)(2,1)}), bf16[16,256,48]{1,2,0:T(8,128)(2,1)}, u32[]{:S(2)}, u32[]{:S(2)}) async-start(bf16[16,256,48]{1,2,0:T(8,128)(2,1)} %bitcast.157), calls=%async_computation.6 | async-start | bytes 786432 | tf_op jit(solution)/shard_map/all_to_all | solution.py:186
  194.2 3.1 %fusion.15 = f32[32,128,1,48]{1,3,0,2:T(8,128)S(1)} fusion(bf16[32,128,1,48]{1,3,0,2:T(8,128)(2,1)S(1)} %copy-done.10, bf16[31,128,1,48]{1,3,0,2:T(8,128)(2,1)S(1)} %copy-done.16, bf16[1,128,1,48]{1,3,0,2:T(8,128)(2,1)} %bitcast.15, f32[32,128,256]{2,1,0:T(8,128)} %get-tuple-element.13, f32[32,128]{1,0:T(8,128)S(1)} %get-tuple-element.12), kind=kOutput, calls=%fused_computation.28 | convolution fusion | flops 105512960 | bytes 5783552 | tf_op jit(solution)/shard_map/nhij,njhd->nihd/dot_general | solution.py:84
  198.0 6.9 %fusion.7 = bf16[16,1,128,256]{3,0,2,1:T(8,128)(2,1)} fusion(f32[32,128,256]{2,1,0:T(8,128)} %copy-done.1, s32[32]{0:T(128)S(1)} %copy-done.25), kind=kOutput, calls=%fused_computation.12 | convolution fusion | flops 201851392 | bytes 5243008 | tf_op jit(solution)/shard_map/nt,nhij->thij/dot_general | solution.py:177
  207.6 5.9 %all-to-all-start.8 = ((bf16[16,256,48]{1,2,0:T(8,128)(2,1)}), bf16[16,256,48]{1,2,0:T(8,128)(2,1)S(1)}, u32[]{:S(2)}, u32[]{:S(2)}) async-start(bf16[16,256,48]{1,2,0:T(8,128)(2,1)} %fusion.38), calls=%async_computation.8 | async-start | bytes 786432 | tf_op jit(solution)/shard_map/all_to_all | solution.py:188
  213.5 1.9 fusion.70
  218.6 8.6 %all-to-all-done.8 = bf16[16,256,48]{1,2,0:T(8,128)(2,1)S(1)} async-done(((bf16[16,256,48]{1,2,0:T(8,128)(2,1)}), bf16[16,256,48]{1,2,0:T(8,128)(2,1)S(1)}, u32[]{:S(2)}, u32[]{:S(2)}) %all-to-all-start.8) | async-done | bytes 393248 | tf_op jit(solution)/shard_map/all_to_all | solution.py:188
  228.9 73.5 %all-reduce.4.cloned.1.call-done = bf16[16,1,128,256]{3,0,2,1:T(8,128)(2,1)} async-done(((bf16[16,1,128,256]{3,0,2,1:T(8,128)(2,1)}), bf16[16,1,128,256]{3,0,2,1:T(8,128)(2,1)}) %all-reduce.4.cloned.1.call-update) | async-done | bytes 1048592 | tf_op jit(solution)/shard_map/psum | solution.py:180
  302.4 2.9 copy.133
  (134 shorter events, 56.9 us)
Async XLA Ops:
  7.2 14.7 %copy-start = (bf16[768,768]{1,0:T(8,128)(2,1)S(1)}, bf16[768,768]{1,0:T(8,128)(2,1)}, u32[]{:S(2)}) copy-start(bf16[768,768]{1,0:T(8,128)(2,1)} %param.16) | copy-start | bytes 3538948
  8.4 48.3 %copy-start.17 = (f32[256]{0:T(256)}, f32[256]{0:T(256)S(1)}, u32[]{:S(2)}) copy-start(f32[256]{0:T(256)S(1)} %broadcast_multiply_fusion.2) | copy-start | bytes 3076
  9.7 12.2 %copy-start.2 = (bf16[256,768]{1,0:T(8,128)(2,1)S(1)}, bf16[256,768]{1,0:T(8,128)(2,1)}, u32[]{:S(2)}) copy-start(bf16[256,768]{1,0:T(8,128)(2,1)} %param.11) | copy-start | bytes 1179652
  9.7 47.0 %copy-start.21 = (f32[256]{0:T(256)}, f32[256]{0:T(256)S(1)}, u32[]{:S(2)}) copy-start(f32[256]{0:T(256)S(1)} %add_rsqrt_fusion) | copy-start | bytes 3076
  10.4 46.3 %copy-start.19 = (f32[768]{0:T(1024)}, f32[768]{0:T(1024)S(1)}, u32[]{:S(2)}) copy-start(f32[768]{0:T(1024)S(1)} %convert_element_type.142) | copy-start | bytes 9220
  13.3 22.3 %all-to-all-start.1 = ((bf16[256,16,48]{0,2,1:T(8,128)(2,1)}), bf16[256,16,48]{0,2,1:T(8,128)(2,1)S(1)}, u32[]{:S(2)}, u32[]{:S(2)}) async-start(bf16[256,16,48]{0,2,1:T(8,128)(2,1)} %bitcast.6), calls=%async_computation.1 | async-start | bytes 786432 | tf_op jit(solution)/shard_map/all_to_all | solution.py:147
  21.9 17.4 %copy-start.13 = (bf16[768,768]{1,0:T(8,128)(2,1)S(1)}, bf16[768,768]{1,0:T(8,128)(2,1)}, u32[]{:S(2)}) copy-start(bf16[768,768]{1,0:T(8,128)(2,1)} %param.15) | copy-start | bytes 3538948
  35.5 17.5 %all-to-all-start.3 = ((bf16[256,16,48]{0,2,1:T(8,128)(2,1)}), bf16[256,16,48]{0,2,1:T(8,128)(2,1)S(1)}, u32[]{:S(2)}, u32[]{:S(2)}) async-start(bf16[256,16,48]{0,2,1:T(8,128)(2,1)} %bitcast.11), calls=%async_computation.3 | async-start | bytes 786432 | tf_op jit(solution)/shard_map/all_to_all | solution.py:150
  53.0 17.4 %all-to-all-start.4 = ((bf16[256,16,48]{0,2,1:T(8,128)(2,1)}), bf16[256,16,48]{0,2,1:T(8,128)(2,1)S(1)}, u32[]{:S(2)}, u32[]{:S(2)}) async-start(bf16[256,16,48]{0,2,1:T(8,128)(2,1)} %bitcast.13), calls=%async_computation.4 | async-start | bytes 786432 | tf_op jit(solution)/shard_map/all_to_all | solution.py:149
  56.7 17.4 %copy-start.26 = (s32[16]{0:T(128)S(1)}, s32[16]{0:T(128)}, u32[]{:S(2)}) copy-start(s32[16]{0:T(128)} %param.19) | copy-start | bytes 196
  70.4 17.4 %all-to-all-start = ((bf16[256,16,48]{0,2,1:T(8,128)(2,1)}), bf16[256,16,48]{0,2,1:T(8,128)(2,1)S(1)}, u32[]{:S(2)}, u32[]{:S(2)}) async-start(bf16[256,16,48]{0,2,1:T(8,128)(2,1)} %bitcast), calls=%async_computation | async-start | bytes 786432 | tf_op jit(solution)/shard_map/all_to_all | solution.py:148
  74.4 13.5 %copy-start.23 = (s32[16]{0:T(128)}, s32[16]{0:T(128)S(1)}, u32[]{:S(2)}) copy-start(s32[16]{0:T(128)S(1)} %reduce.6) | copy-start | bytes 196
  87.9 26.0 %all-to-all-start.2 = ((bf16[256,16,48]{0,2,1:T(8,128)(2,1)}), bf16[256,16,48]{0,2,1:T(8,128)(2,1)S(1)}, u32[]{:S(2)}, u32[]{:S(2)}) async-start(bf16[256,16,48]{0,2,1:T(8,128)(2,1)} %bitcast.168), calls=%async_computation.2 | async-start | bytes 786432 | tf_op jit(solution)/shard_map/all_to_all | solution.py:151
  101.6 17.5 %copy-start.6 = (bf16[32,128,48]{1,0,2:T(8,128)(2,1)}, bf16[32,128,48]{1,0,2:T(8,128)(2,1)S(1)}, u32[]{:S(2)}) copy-start(bf16[32,128,48]{1,0,2:T(8,128)(2,1)S(1)} %reshape.250) | copy-start | bytes 1179652
  105.5 5.0 %copy-start.8 = (bf16[32,128,1,48]{1,3,0,2:T(8,128)(2,1)}, bf16[32,128,1,48]{1,3,0,2:T(8,128)(2,1)S(1)}, u32[]{:S(2)}) copy-start(bf16[32,128,1,48]{1,3,0,2:T(8,128)(2,1)S(1)} %copy.115) | copy-start | bytes 1179652
  107.0 27.4 %collective-permute-start.1 = (bf16[128,48]{0,1:T(8,128)(2,1)}, bf16[128,48]{0,1:T(8,128)(2,1)}, u32[]{:S(2)}, u32[]{:S(2)}) collective-permute-start(bf16[128,48]{0,1:T(8,128)(2,1)} %slice.78), channel_id=1, source_target_pairs={{0,16},{16,32},{32,48},{48,64},{64,80},{80,96},{96,112},{112,128},... | collective-permute-start | bytes 36872 | tf_op jit(solution)/shard_map/ppermute | solution.py:17
  110.5 8.6 %collective-permute-start = (bf16[128,48]{0,1:T(8,128)(2,1)S(1)}, bf16[128,48]{0,1:T(8,128)(2,1)}, u32[]{:S(2)}, u32[]{:S(2)}) collective-permute-start(bf16[128,48]{0,1:T(8,128)(2,1)S(1)} %slice.76), channel_id=1, source_target_pairs={{0,16},{16,32},{32,48},{48,64},{64,80},{80,96},{96,112},{112,128},... | collective-permute-start | bytes 36872 | tf_op jit(solution)/shard_map/ppermute | solution.py:17
  113.9 3.9 %copy-start.4 = (bf16[256,16,48]{0,2,1:T(8,128)(2,1)}, bf16[256,16,48]{0,2,1:T(8,128)(2,1)S(1)}, u32[]{:S(2)}) copy-start(bf16[256,16,48]{0,2,1:T(8,128)(2,1)S(1)} %all-to-all-done.2) | copy-start | bytes 1179652
  142.1 21.0 %collective-permute-start.3 = (bf16[128,48]{0,1:T(8,128)(2,1)}, bf16[128,48]{0,1:T(8,128)(2,1)}, u32[]{:S(2)}, u32[]{:S(2)}) collective-permute-start(bf16[128,48]{0,1:T(8,128)(2,1)} %fusion.52), channel_id=1, source_target_pairs={{16,0},{32,16},{48,32},{64,48},{80,64},{96,80},{112,96},{128,112},... | collective-permute-start | bytes 36872 | tf_op jit(solution)/shard_map/ppermute | solution.py:17
  150.8 21.0 %all-to-all-start.5 = ((bf16[16,256,48]{1,2,0:T(8,128)(2,1)}), bf16[16,256,48]{1,2,0:T(8,128)(2,1)}, u32[]{:S(2)}, u32[]{:S(2)}) async-start(bf16[16,256,48]{1,2,0:T(8,128)(2,1)} %copy.119), calls=%async_computation.5 | async-start | bytes 786432 | tf_op jit(solution)/shard_map/all_to_all | solution.py:185
  160.1 17.5 %collective-permute-start.2 = (bf16[128,48]{0,1:T(8,128)(2,1)}, bf16[128,48]{0,1:T(8,128)(2,1)}, u32[]{:S(2)}, u32[]{:S(2)}) collective-permute-start(bf16[128,48]{0,1:T(8,128)(2,1)} %fusion.51), channel_id=1, source_target_pairs={{16,0},{32,16},{48,32},{64,48},{80,64},{96,80},{112,96},{128,112},... | collective-permute-start | bytes 36872 | tf_op jit(solution)/shard_map/ppermute | solution.py:17
  171.8 17.9 %all-to-all-start.7 = ((bf16[16,256,48]{1,2,0:T(8,128)(2,1)}), bf16[16,256,48]{1,2,0:T(8,128)(2,1)}, u32[]{:S(2)}, u32[]{:S(2)}) async-start(bf16[16,256,48]{1,2,0:T(8,128)(2,1)} %bitcast.169), calls=%async_computation.7 | async-start | bytes 786432 | tf_op jit(solution)/shard_map/all_to_all | solution.py:187
  177.3 16.9 %copy-start.10 = (bf16[32,128,1,48]{1,3,0,2:T(8,128)(2,1)S(1)}, bf16[32,128,1,48]{1,3,0,2:T(8,128)(2,1)}, u32[]{:S(2)}) copy-start(bf16[32,128,1,48]{1,3,0,2:T(8,128)(2,1)} %copy-done.8) | copy-start | bytes 1179652
  177.3 16.9 %copy-start.16 = (bf16[31,128,1,48]{1,3,0,2:T(8,128)(2,1)S(1)}, bf16[31,128,1,48]{1,3,0,2:T(8,128)(2,1)}, u32[]{:S(2)}) copy-start(bf16[31,128,1,48]{1,3,0,2:T(8,128)(2,1)} %slice.79) | copy-start | bytes 1142788
  189.7 17.9 %all-to-all-start.6 = ((bf16[16,256,48]{1,2,0:T(8,128)(2,1)}), bf16[16,256,48]{1,2,0:T(8,128)(2,1)}, u32[]{:S(2)}, u32[]{:S(2)}) async-start(bf16[16,256,48]{1,2,0:T(8,128)(2,1)} %bitcast.157), calls=%async_computation.6 | async-start | bytes 786432 | tf_op jit(solution)/shard_map/all_to_all | solution.py:186
  193.9 108.5 %all-reduce.4.cloned.1.call-start = ((), (), s32[]{:S(2)}) async-start(), calls=%async_computation.9 | async-start | bytes 2097152 | tf_op jit(solution)/shard_map/psum | solution.py:180
  198.0 6.9 %copy-start.5 = (bf16[256,16,48]{0,2,1:T(8,128)(2,1)S(1)}, bf16[256,16,48]{0,2,1:T(8,128)(2,1)}, u32[]{:S(2)}) copy-start(bf16[256,16,48]{0,2,1:T(8,128)(2,1)} %copy-done.4) | copy-start | bytes 1179652
  206.2 9.2 %copy-start.12 = (bf16[768,768]{1,0:T(8,128)(2,1)S(1)}, bf16[768,768]{1,0:T(8,128)(2,1)}, u32[]{:S(2)}) copy-start(bf16[768,768]{1,0:T(8,128)(2,1)} %param.14) | copy-start | bytes 3538948
  207.6 19.6 %all-to-all-start.8 = ((bf16[16,256,48]{1,2,0:T(8,128)(2,1)}), bf16[16,256,48]{1,2,0:T(8,128)(2,1)S(1)}, u32[]{:S(2)}, u32[]{:S(2)}) async-start(bf16[16,256,48]{1,2,0:T(8,128)(2,1)} %fusion.38), calls=%async_computation.8 | async-start | bytes 786432 | tf_op jit(solution)/shard_map/all_to_all | solution.py:188
  217.0 10.1 %copy-start.18 = (f32[256]{0:T(256)S(1)}, f32[256]{0:T(256)}, u32[]{:S(2)}) copy-start(f32[256]{0:T(256)} %copy-done.17) | copy-start | bytes 3076
  217.0 10.1 %copy-start.20 = (f32[768]{0:T(1024)S(1)}, f32[768]{0:T(1024)}, u32[]{:S(2)}) copy-start(f32[768]{0:T(1024)} %copy-done.19) | copy-start | bytes 9220
  217.1 10.1 %copy-start.22 = (f32[256]{0:T(256)S(1)}, f32[256]{0:T(256)}, u32[]{:S(2)}) copy-start(f32[256]{0:T(256)} %copy-done.21) | copy-start | bytes 3076
  (9 other events, 18.8 us)
Sparse Core Ops, SparseCore 0:
  205.0 97.3 all-reduce.3
where the time goes:
time: 315 us; the launch traced here: 312 us
  waiting for transfers between devices  143 us (45%)
  starting transfers between devices  56.8 us (18%)
  matrix products  47.2 us (15%)
  local copies, waits for them, and re-layouts  34.3 us (11%)
  other arithmetic  16.1 us (5%)
  between operations  14.7 us (5%)
    psum x1, waiting for transfers between devices, shards(): lax.psum(local_tiles.astype(jnp.bfloat16), 'seq').astype(jnp.float32)  73.5 us
    sub x1, matrix products, attention_pass(): weights = jnp.where(mask, jnp.exp(scores - top), 0.0)  12.2 us
    all_to_all x1, waiting for transfers between devices, shards(): lax.all_to_all(queries, 'head', split_axis=1, concat_axis=0, tiled=True)  12.2 us
    ppermute x4, starting transfers between devices, passed_along(): return lax.ppermute(array, axis, pairs)  11.8 us
    all_to_all x1, waiting for transfers between devices, shards(): lax.all_to_all(values, 'head', split_axis=1, concat_axis=0, tiled=True)  11 us
    all_to_all x1, waiting for transfers between devices, shards(): lax.all_to_all(d_values, 'head', split_axis=0, concat_axis=1, tiled=True)  10.6 us
    all_to_all x1, waiting for transfers between devices, shards(): lax.all_to_all(gate_input, 'head', split_axis=1, concat_axis=0, tiled=True)  10.6 us
    all_to_all x1, starting transfers between devices, shards(): lax.all_to_all(queries, 'head', split_axis=1, concat_axis=0, tiled=True)  8.57 us
  transfers between devices with their start and end apart: 14, of which 9 were waited for; matrix products, arithmetic and copies ran while one was open for 25% of the time, Pallas kernels for 0%

commit v1 on v0

v1 whole, which is shorter than its diff:
```python
import functools
import math

import jax
import jax.numpy as jnp
from jax import lax
from jax.experimental import pallas as pl
from jax.experimental.pallas import tpu as pltpu
from jax.sharding import PartitionSpec as P

MESH = pl.DeviceIdType.MESH
F32 = jnp.float32
BF16 = jnp.bfloat16
EPS = 1e-05
UNSEEN = -1e30
BLOCK = 128
PAIR = 2 * BLOCK


def mm(a, b, dims):
    return lax.dot_general(a, b, (dims, ((), ())), preferred_element_type=F32)


def kernel(
    H, S, DH,
    act_ref, gain_ref, dout_ref, wq_hbm, wk_hbm, wv_hbm, wg_hbm, wo_hbm, bias_ref,
    lengths_ref, tiles_ref, chain_ref, last_ref,
    dact_ref, dbias_ref,
    wq, wk, wv, wg, wo, normed, scaled, inverse, gin, dmix, send, recv, res, got,
    own, nxt, chain, hotq, hotk, edge_out, edge_in, parts, parts_in, summed, dnorm,
    w_sem, f_send, f_recv, b_send, b_recv, r_send, r_recv, a_send, a_recv, e_send, e_recv,
):
    s, h = lax.axis_index("seq"), lax.axis_index("head")
    D = H * DH
    half_heads = H // 2
    half_cols = half_heads * DH
    scale = 1.0 / math.sqrt(DH)
    q_rows, k_rows, v_rows, g_rows = (pl.ds(i * DH, DH) for i in range(4))
    kv_rows = pl.ds(DH, 2 * DH)
    last_block = pl.ds(BLOCK, BLOCK)

    def wrap(i, n):
        return lax.rem(i + n, n)

    barrier = pltpu.get_barrier_semaphore()
    for o in range(1, H):
        pl.semaphore_signal(barrier, inc=1, device_id=(s, wrap(h + o, H)), device_id_type=MESH)
    for o in range(1, S):
        pl.semaphore_signal(barrier, inc=1, device_id=(wrap(s + o, S), h), device_id_type=MESH)

    loads = [
        pltpu.make_async_copy(a, b, w_sem.at[i])
        for i, (a, b) in enumerate(
            ((wq_hbm, wq), (wk_hbm, wk), (wv_hbm, wv), (wg_hbm, wg), (wo_hbm, wo))
        )
    ]
    for load in loads:
        load.start()

    gain = gain_ref[...].astype(F32)
    x = act_ref[...].astype(F32)
    centred = x - jnp.mean(x, axis=1, keepdims=True)
    inv = lax.rsqrt(jnp.mean(centred * centred, axis=1, keepdims=True) + EPS)
    xhat = centred * inv
    scaled[...] = xhat
    inverse[...] = jnp.broadcast_to(inv, inverse.shape)
    normed[...] = (xhat * gain).astype(BF16)

    def forward_copy(t):
        return pltpu.make_async_remote_copy(
            send.at[t], recv.at[h + 1], f_send.at[t], f_recv.at[h],
            device_id=(s, t), device_id_type=MESH,
        )

    def forward_arrival(j):
        return pltpu.make_async_remote_copy(
            send.at[j], recv.at[j + 1], f_send.at[j], f_recv.at[j],
            device_id=(s, j), device_id_type=MESH,
        )

    own_copy = pltpu.make_async_copy(send.at[h], recv.at[h + 1], f_recv.at[h])
    offsets = []
    for i in range(H - 1):
        offsets.append(-(i // 2 + 1) if i % 2 == 0 else i // 2 + 1)

    def by_head(product):
        return product.T.astype(BF16).reshape(half_heads, DH, PAIR)

    my_half = h // half_heads
    for turn in range(2):
        half = my_half if turn == 0 else 1 - my_half
        cols = pl.ds(pl.multiple_of(half * half_cols, 128), half_cols)
        heads = pl.ds(half * half_heads, half_heads)
        rows_in = normed[...]
        for i, (w, rows) in enumerate(((wq, q_rows), (wk, k_rows), (wv, v_rows))):
            if turn == 0:
                loads[i].wait()
            send[heads, rows, :] = by_head(mm(rows_in, w[:, cols], ((1,), (0,))))
        if turn == 0:
            loads[3].wait()
            loads[4].wait()
        gate_in = by_head(mm(rows_in, wg[:, cols], ((1,), (0,))))
        mixed = mm(wo[cols, :], dout_ref[...], ((1,), (1,))).astype(BF16)
        mixed = mixed.reshape(half_heads, DH, PAIR)
        gin[heads] = gate_in
        dmix[heads] = mixed
        gate = jax.nn.sigmoid(gate_in.astype(F32))
        send[heads, g_rows, :] = (mixed.astype(F32) * gate).astype(BF16)
        if turn == 0:
            pl.semaphore_wait(barrier, H + S - 2)
            own_copy.start()
        for off in offsets:
            t = wrap(h + off, H)

            @pl.when(t // half_heads == half)
            def _(t=t):
                forward_copy(t).start()

    crops = lengths_ref.shape[0]
    row = lax.broadcasted_iota(jnp.int32, (crops, PAIR), 0)
    lane = lax.broadcasted_iota(jnp.int32, (crops, PAIR), 1)
    low = jnp.zeros((crops, PAIR), jnp.int32)
    high = jnp.zeros((crops, PAIR), jnp.int32)
    total = jnp.int32(0)
    for c in range(crops):
        low = jnp.where(row == c, total, low)
        total = total + lengths_ref[c]
        high = jnp.where(row == c, total, high)
    for j in range(H + 1):
        pos = (s * H + j - 1) * PAIR + lane
        inside = (pos >= low) & (pos < high)
        hotq[j] = jnp.where(inside, 1.0, 0.0).astype(BF16)
        hotk[j] = jnp.where(inside, 0.0, UNSEEN).astype(BF16)

    def clear(n, carry):
        chain[n] = jnp.zeros((BLOCK, PAIR), F32)
        return carry

    lax.fori_loop(0, 2 * H, clear, 0)

    @pl.when(s == 0)
    def _():
        recv[0] = jnp.zeros((4 * DH, PAIR), BF16)

    key_edge = pltpu.make_async_remote_copy(
        recv.at[H, kv_rows, last_block], recv.at[0, kv_rows, last_block],
        e_send.at[0], e_recv.at[0],
        device_id=(wrap(s + 1, S), h), device_id_type=MESH,
    )
    grad_edge = pltpu.make_async_remote_copy(
        edge_out, edge_in, e_send.at[1], e_recv.at[1],
        device_id=(wrap(s + S - 1, S), h), device_id_type=MESH,
    )

    def back_copy(t):
        return pltpu.make_async_remote_copy(
            res.at[t], got.at[h], b_send.at[t], b_recv.at[h],
            device_id=(s, t), device_id_type=MESH,
        )

    def back_arrival(j):
        return pltpu.make_async_remote_copy(
            res.at[j], got.at[j], b_send.at[j], b_recv.at[j],
            device_id=(s, j), device_id_type=MESH,
        )

    own_back = pltpu.make_async_copy(res.at[h], got.at[h], b_recv.at[h])

    def finish(f):
        later = nxt[f + 1]
        total = own[f]
        res[f, pl.ds(2 * DH, 2 * DH), pl.ds(0, BLOCK)] = total[:, :BLOCK].astype(BF16)
        res[f, pl.ds(2 * DH, 2 * DH), last_block] = (total[:, BLOCK:] + later).astype(BF16)

        @pl.when(f == h)
        def _():
            own_back.start()

        @pl.when(f != h)
        def _():
            back_copy(f).start()

    own_copy.wait()

    @pl.when((h == H - 1) & (s < S - 1))
    def _():
        key_edge.start()

    def attend(j, b, slot):
        n = 2 * j + b
        lanes = pl.ds(b * BLOCK, BLOCK)
        q = recv[j + 1, q_rows, lanes]
        g = recv[j + 1, g_rows, lanes]
        if b == 0:
            k = jnp.concatenate([recv[j, k_rows, last_block], recv[j + 1, k_rows, lanes]], axis=1)
            v = jnp.concatenate([recv[j, v_rows, last_block], recv[j + 1, v_rows, lanes]], axis=1)
            hot = jnp.concatenate([hotk[j, :, last_block], hotk[j + 1, :, lanes]], axis=1)
        else:
            k = recv[j + 1, k_rows, :]
            v = recv[j + 1, v_rows, :]
            hot = hotk[j + 1]
        q_all = jnp.concatenate([q, hotq[j + 1, :, lanes]], axis=0)
        k_all = jnp.concatenate([k, hot], axis=0)
        scores = mm(q_all, k_all, ((0,), (0,))) * scale + bias_ref[tiles_ref[n]].astype(F32)
        weights = jnp.exp(scores - jnp.max(scores, axis=1, keepdims=True))
        probs = weights * (1.0 / jnp.sum(weights, axis=1, keepdims=True))
        probs_low = probs.astype(BF16)
        d_probs = mm(g, v, ((0,), (0,)))
        weighted = probs * d_probs
        d_scores = weighted - probs * jnp.sum(weighted, axis=1, keepdims=True)
        d_low = d_scores.astype(BF16)
        res[j, pl.ds(0, DH), lanes] = mm(v, probs_low, ((1,), (1,))).astype(BF16)
        res[j, pl.ds(DH, DH), lanes] = (mm(k, d_low, ((1,), (1,))) * scale).astype(BF16)
        before = chain_ref[n]
        kept = jnp.where(before >= 0, chain[jnp.maximum(before, 0)], 0.0)
        chain[slot] = kept + d_scores
        d_k = mm(q, d_low, ((1,), (0,))) * scale
        d_v = mm(g, probs_low, ((1,), (0,)))
        return d_k, d_v

    def step(i, carry):
        up = lax.rem(i, 2) == 0
        far = i // 2
        j = wrap(h + jnp.where(up, 1 + far, -far), H)
        arrived = jnp.where(up, j, wrap(j + H - 1, H))

        @pl.when(i < H - 1)
        def _():
            forward_arrival(arrived).wait_recv()

            @pl.when((arrived == H - 1) & (s < S - 1))
            def _():
                key_edge.start()

        @pl.when((j == 0) & (s > 0))
        def _():
            key_edge.wait_recv()

        first_k, first_v = attend(j, 0, 2 * i)
        second_k, second_v = attend(j, 1, 2 * i + 1)
        nxt[j, pl.ds(0, DH), :] = first_k[:, :BLOCK]
        nxt[j, pl.ds(DH, DH), :] = first_v[:, :BLOCK]
        own[j, pl.ds(0, DH), pl.ds(0, BLOCK)] = first_k[:, BLOCK:] + second_k[:, :BLOCK]
        own[j, pl.ds(DH, DH), pl.ds(0, BLOCK)] = first_v[:, BLOCK:] + second_v[:, :BLOCK]
        own[j, pl.ds(0, DH), last_block] = second_k[:, BLOCK:]
        own[j, pl.ds(DH, DH), last_block] = second_v[:, BLOCK:]

        @pl.when((j == 0) & (s > 0))
        def _():
            edge_out[...] = nxt[0].astype(BF16)
            grad_edge.start()

        f = jnp.where(up, wrap(j + H - 1, H), j)

        @pl.when((i > 0) & (f != H - 1))
        def _():
            finish(f)

        return carry

    lax.fori_loop(0, H, step, 0)

    def part_copy(t):
        return pltpu.make_async_remote_copy(
            parts.at[t], parts_in.at[s], r_send.at[t], r_recv.at[s],
            device_id=(t, h), device_id_type=MESH,
        )

    def part_arrival(j):
        return pltpu.make_async_remote_copy(
            parts.at[j], parts_in.at[j], r_send.at[j], r_recv.at[j],
            device_id=(j, h), device_id_type=MESH,
        )

    own_part = pltpu.make_async_copy(parts.at[s], parts_in.at[s], r_recv.at[s])

    def part(o, carry):
        t = wrap(s + o, S)
        at = last_ref[t]
        parts[t] = jnp.where(at >= 0, chain[jnp.maximum(at, 0)], 0.0).astype(BF16)

        @pl.when(t == s)
        def _():
            own_part.start()

        @pl.when(t != s)
        def _():
            part_copy(t).start()

        return carry

    lax.fori_loop(1, S + 1, part, 0)

    opposite = wrap(h + H // 2, H)

    @pl.when(opposite != H - 1)
    def _():
        finish(opposite)

    @pl.when(s < S - 1)
    def _():
        grad_edge.wait_recv()
        nxt[H] = edge_in[...].astype(F32)

    @pl.when(s == S - 1)
    def _():
        nxt[H] = jnp.zeros((2 * DH, BLOCK), F32)

    finish(jnp.int32(H - 1))

    own_part.wait()
    for o in range(1, S):
        part_arrival(wrap(s + o, S)).wait_recv()
    half_block = BLOCK // 2
    for piece in range(2):
        rows = pl.ds(piece * half_block, half_block)
        sums = parts_in[0, rows, :].astype(F32)
        for j in range(1, S):
            sums = sums + parts_in[j, rows, :].astype(F32)
        summed[rows, :] = sums.astype(BF16)

    def sum_copy(t):
        return pltpu.make_async_remote_copy(
            summed, dbias_ref.at[s], a_send.at[t], a_recv.at[s],
            device_id=(t, h), device_id_type=MESH,
        )

    def sum_arrival(j):
        return pltpu.make_async_remote_copy(
            summed, dbias_ref.at[j], a_send.at[j], a_recv.at[j],
            device_id=(j, h), device_id_type=MESH,
        )

    own_sum = pltpu.make_async_copy(summed, dbias_ref.at[s], a_recv.at[s])
    own_sum.start()
    for o in range(1, S):
        sum_copy(wrap(s + o, S)).start()

    own_back.wait()
    for o in range(1, H):
        back_arrival(wrap(h + o, H)).wait_recv()
    gate = jax.nn.sigmoid(gin[...].astype(F32))
    attended = got[:, pl.ds(0, DH), :].astype(F32)
    d_gate = (dmix[...].astype(F32) * attended * gate * (1.0 - gate)).astype(BF16).reshape(D, PAIR)
    got[:, pl.ds(0, DH), :] = d_gate.reshape(H, DH, PAIR)
    chunk = 256

    def product(m, carry):
        rows = pl.ds(pl.multiple_of(m * chunk, chunk), chunk)
        acc = jnp.zeros((chunk, PAIR), F32)
        for i, w in enumerate((wg, wq, wk, wv)):
            grads = got[:, pl.ds(i * DH, DH), :].reshape(D, PAIR)
            acc = acc + mm(w[rows, :], grads, ((1,), (0,)))
        dnorm[rows, :] = acc
        return carry

    lax.fori_loop(0, D // chunk, product, 0)
    for piece in range(2):
        rows = pl.ds(piece * BLOCK, BLOCK)
        g = dnorm[:, rows].T * gain
        xhat = scaled[rows, :]
        centre = jnp.mean(g, axis=1, keepdims=True)
        along = jnp.mean(g * xhat, axis=1, keepdims=True)
        dact_ref[rows, :] = (inverse[rows, :1] * (g - centre - xhat * along)).astype(BF16)

    own_sum.wait()
    for o in range(1, S):
        sum_arrival(wrap(s + o, S)).wait_recv()

    for o in range(1, H):
        t = wrap(h + o, H)
        forward_copy(t).wait_send()
        back_copy(t).wait_send()
    for o in range(1, S):
        t = wrap(s + o, S)
        part_copy(t).wait_send()
        sum_copy(t).wait_send()

    @pl.when(s < S - 1)
    def _():
        key_edge.wait_send()

    @pl.when(s > 0)
    def _():
        grad_edge.wait_send()


def shards(H, S, activations, ln_gain, w_query, w_key, w_value, w_gate, w_out, bias_tiles,
           crop_lengths, tile_index, d_out):
    rows, D = activations.shape
    DH = D // H
    tiles = bias_tiles.shape[0]
    crops = crop_lengths.shape[0]
    h = lax.axis_index("head").astype(jnp.int32)
    n = jnp.arange(2 * H, dtype=jnp.int32)
    above = jnp.remainder(n // 2 - h, H)
    below = jnp.remainder(h - n // 2, H)
    turn = jnp.where((above >= 1) & (above <= H // 2), 2 * (above - 1), 2 * below + 1)
    slot = 2 * turn + n % 2
    same = tile_index[:, None] == tile_index[None, :]
    chain = jnp.max(jnp.where(same & (slot[None, :] < slot[:, None]), slot[None, :], -1), axis=1)
    here = jnp.arange(tiles, dtype=jnp.int32)[:, None] == tile_index[None, :]
    last = jnp.max(jnp.where(here, slot[None, :], -1), axis=1)

    vmem = pl.BlockSpec(memory_space=pltpu.VMEM)
    smem = pl.BlockSpec(memory_space=pltpu.SMEM)
    hbm = pl.BlockSpec(memory_space=pl.ANY)
    dma = pltpu.SemaphoreType.DMA
    d_act, d_bias = pl.pallas_call(
        functools.partial(kernel, H, S, DH),
        out_shape=(
            jax.ShapeDtypeStruct((rows, D), BF16),
            jax.ShapeDtypeStruct((tiles, BLOCK, PAIR), BF16),
        ),
        in_specs=[vmem, vmem, vmem, hbm, hbm, hbm, hbm, hbm, vmem, smem, smem, smem, smem],
        out_specs=(vmem, vmem),
        scratch_shapes=[
            *[pltpu.VMEM((D, D), BF16) for _ in range(5)],
            pltpu.VMEM((rows, D), BF16),
            pltpu.VMEM((rows, D), F32),
            pltpu.VMEM((rows, 128), F32),
            pltpu.VMEM((H, DH, PAIR), BF16),
            pltpu.VMEM((H, DH, PAIR), BF16),
            pltpu.VMEM((H, 4 * DH, PAIR), BF16),
            pltpu.VMEM((H + 1, 4 * DH, PAIR), BF16),
            pltpu.VMEM((H, 4 * DH, PAIR), BF16),
            pltpu.VMEM((H, 4 * DH, PAIR), BF16),
            pltpu.VMEM((H, 2 * DH, PAIR), F32),
            pltpu.VMEM((H + 1, 2 * DH, BLOCK), F32),
            pltpu.VMEM((2 * H, BLOCK, PAIR), F32),
            pltpu.VMEM((H + 1, crops, PAIR), BF16),
            pltpu.VMEM((H + 1, crops, PAIR), BF16),
            pltpu.VMEM((2 * DH, BLOCK), BF16),
            pltpu.VMEM((2 * DH, BLOCK), BF16),
            pltpu.VMEM((tiles, BLOCK, PAIR), BF16),
            pltpu.VMEM((tiles, BLOCK, PAIR), BF16),
            pltpu.VMEM((BLOCK, PAIR), BF16),
            pltpu.VMEM((D, PAIR), F32),
            dma((5,)),
            *[dma((H,)) for _ in range(4)],
            *[dma((S,)) for _ in range(4)],
            dma((2,)),
            dma((2,)),
        ],
        compiler_params=pltpu.CompilerParams(
            collective_id=0, has_side_effects=True, vmem_limit_bytes=50 * 2**20
        ),
    )(
        activations, ln_gain.reshape(1, D), d_out, w_query, w_key, w_value, w_gate, w_out,
        bias_tiles.reshape(tiles, BLOCK, PAIR), crop_lengths, tile_index, chain, last,
    )
    return d_act, d_bias.astype(F32).reshape(tiles, 1, BLOCK, PAIR)


def solution(mesh):
    return jax.shard_map(
        functools.partial(shards, mesh.shape["head"], mesh.shape["seq"]),
        mesh=mesh,
        in_specs=(
            P(("seq", "head"), None),
            P(),
            P(),
            P(),
            P(),
            P(),
            P(),
            P(None, "head", None, None),
            P(),
            P("seq"),
            P(("seq", "head"), None),
        ),
        out_specs=(P(("seq", "head"), None), P(None, "head", None, None)),
        check_vma=False,
    )
```

time: 315 us -> 95.7 us (0.30)
  the two profiles are of different devices: /device:TPU:8 before, /device:TPU:32 now
where the time goes in v1:
time: 95.7 us; the launch traced here: 95.4 us
  Pallas kernels  85.6 us (89%)
  local copies, waits for them, and re-layouts  5.96 us (6%)
  other arithmetic  3.25 us (3%)
    pallas_call x1, Pallas kernels, shards(): pl.pallas_call(functools.partial(kernel, H, S, DH), out_shape=(jax.ShapeD...  85.6 us
    unnamed x11, local copies, waits for them, and re-layouts  5.27 us

profile of v1, /device:TPU:32, one launch (start us, length us, event | category | flops | bytes accessed | tf_op | source)
XLA Modules:
  0.0 95.4 jit_solution(1402869325240210772)
XLA Ops:
  0.7 0.8 select_reduce_fusion.1.last_ref
  1.4 0.9 select_reduce_fusion.chain_ref
  2.3 0.7 reshape.126.gain_ref
  3.0 0.0 copy-start
  3.0 1.2 %copy-done = bf16[16,1,128,256]{3,2,1,0:T(8,128)(2,1)S(1)} copy-done((bf16[16,1,128,256]{3,2,1,0:T(8,128)(2,1)S(1)}, bf16[16,1,128,256]{3,2,1,0:T(8,128)(2,1)}, u32[]{:S(2)}) %copy-start) | copy-done | bytes 1048600
  4.3 0.0 copy-start.1
  4.3 1.0 %copy-done.1 = bf16[256,768]{1,0:T(8,128)(2,1)S(1)} copy-done((bf16[256,768]{1,0:T(8,128)(2,1)S(1)}, bf16[256,768]{1,0:T(8,128)(2,1)}, u32[]{:S(2)}) %copy-start.1) | copy-done | bytes 393240
  5.3 0.0 copy-start.2
  5.3 1.0 %copy-done.2 = bf16[256,768]{1,0:T(8,128)(2,1)S(1)} copy-done((bf16[256,768]{1,0:T(8,128)(2,1)S(1)}, bf16[256,768]{1,0:T(8,128)(2,1)}, u32[]{:S(2)}) %copy-start.2) | copy-done | bytes 393240
  6.3 0.0 copy-start.3
  6.3 0.7 copy-done.3
  6.9 0.0 copy-start.4
  6.9 0.7 copy-done.4
  7.6 85.6 %shard_map.122 = (bf16[256,768]{1,0:T(8,128)(2,1)S(1)}, bf16[16,128,256]{2,1,0:T(8,128)(2,1)S(1)}) custom-call(bf16[256,768]{1,0:T(8,128)(2,1)S(1)} %copy-done.1, bf16[1,768]{1,0:T(2,128)(2,1)S(1)} %reshape.126.gain_ref, bf16[256,768]{1,0:T(8,128)(2,1)S(1)} %copy-done.2, bf16[768,768]{1,0:T(8,128)(2,1)} %wq_hbm.1, bf16[768,768]{1,0:T(8,128)(2,1)} %wk_hbm.1, ...), custom_call_target="tpu_custom_call" | custom-call | tf_op jit(solution)/shard_map/pallas_call | solution.py:409
  93.2 1.5 %bitcast_convert_fusion = f32[16,1,128,256]{3,2,1,0:T(8,128)} fusion(bf16[16,128,256]{2,1,0:T(8,128)(2,1)S(1)} %get-tuple-element.5), kind=kLoop, calls=%fused_computation | loop fusion | flops 524288 | bytes 3145728
  94.7 0.7 copy.16
  (1 shorter events, 0.0 us)
Async XLA Ops:
  3.0 1.2 %copy-start = (bf16[16,1,128,256]{3,2,1,0:T(8,128)(2,1)S(1)}, bf16[16,1,128,256]{3,2,1,0:T(8,128)(2,1)}, u32[]{:S(2)}) copy-start(bf16[16,1,128,256]{3,2,1,0:T(8,128)(2,1)} %param.18) | copy-start | bytes 3145732
  4.3 1.0 %copy-start.1 = (bf16[256,768]{1,0:T(8,128)(2,1)S(1)}, bf16[256,768]{1,0:T(8,128)(2,1)}, u32[]{:S(2)}) copy-start(bf16[256,768]{1,0:T(8,128)(2,1)} %act_ref.1) | copy-start | bytes 1179652
  5.3 1.0 %copy-start.2 = (bf16[256,768]{1,0:T(8,128)(2,1)S(1)}, bf16[256,768]{1,0:T(8,128)(2,1)}, u32[]{:S(2)}) copy-start(bf16[256,768]{1,0:T(8,128)(2,1)} %dout_ref.1) | copy-start | bytes 1179652
  6.3 0.7 copy-start.3
  6.9 0.7 copy-start.4

commit v2 on v1

v2 whole, which is shorter than its diff:
```python
import functools
import math

import jax
import jax.numpy as jnp
from jax import lax
from jax.experimental import pallas as pl
from jax.experimental.pallas import tpu as pltpu
from jax.sharding import PartitionSpec as P

MESH = pl.DeviceIdType.MESH
F32 = jnp.float32
BF16 = jnp.bfloat16
EPS = 1e-05
UNSEEN = -1e30
BLOCK = 128
PAIR = 2 * BLOCK


def mm(a, b, dims):
    return lax.dot_general(a, b, (dims, ((), ())), preferred_element_type=F32)


def kernel(
    H, S, DH,
    act_hbm, gain_ref, dout_hbm, wq_hbm, wk_hbm, wv_hbm, wg_hbm, wo_hbm, bias_hbm,
    lengths_ref, tiles_ref,
    dact_ref, dbias_ref,
    act, dout, bias, far_bias, order, wq, wk, wv, wg, wo, normed, scaled, inverse, gin, dmix,
    send, recv, res, got, own, nxt, chain, hotq, hotk, edge_out, edge_in,
    parts, first_a, first_b, mid_a, mid_b, second_a, second_b, crossed, dnorm, gated,
    w_sem, f_send, f_recv, b_send, b_recv, k_send, k_recv, e_send, e_recv, c_send, c_recv,
    g_send, g_recv, r_send, r_recv, a_send, a_recv,
):
    s, h = lax.axis_index("seq"), lax.axis_index("head")
    side = math.isqrt(S)
    planes = H // 2
    sx, sy = s // side, lax.rem(s, side)
    z, c = h // 2, lax.rem(h, 2)
    D = H * DH
    half_heads = H // 2
    half_cols = half_heads * DH
    scale = 1.0 / math.sqrt(DH)
    q_rows, k_rows, v_rows, g_rows = (pl.ds(i * DH, DH) for i in range(4))
    kv_rows = pl.ds(DH, 2 * DH)
    last_block = pl.ds(BLOCK, BLOCK)
    upper, lower = pl.ds(0, BLOCK // 2), pl.ds(BLOCK // 2, BLOCK // 2)
    near, far = 5, 3
    starts = {near: 0, far: 2 * near + 1}
    total_slots = 2 * near + 2 * far + 2
    wraps = {near: total_slots, far: total_slots + 1}
    nxt_wraps = {near: total_slots + 1, far: total_slots + 2}

    def wrap(i, n):
        return lax.rem(i + n, n)

    other = wrap(z + planes // 2, planes)
    far_head = 2 * other + c
    heads_of = {near: h, far: far_head}

    def remote(src, dst, a, b, device):
        return pltpu.make_async_remote_copy(
            src, dst, a, b, device_id=device, device_id_type=MESH
        )

    mine = pl.ds(pl.multiple_of(h // half_heads * half_cols, 128), half_cols)
    rest = pl.ds(pl.multiple_of((1 - h // half_heads) * half_cols, 128), half_cols)
    loads = [pltpu.make_async_copy(act_hbm, act, w_sem.at[0])]
    for turn, cols in enumerate((mine, rest)):
        for i, (a, b) in enumerate(((wq_hbm, wq), (wk_hbm, wk), (wv_hbm, wv), (wg_hbm, wg))):
            loads.append(
                pltpu.make_async_copy(a.at[:, cols], b.at[:, cols], w_sem.at[1 + 5 * turn + i])
            )
        loads.append(
            pltpu.make_async_copy(wo_hbm.at[cols, :], wo.at[cols, :], w_sem.at[5 + 5 * turn])
        )
    dout_load = pltpu.make_async_copy(dout_hbm, dout, w_sem.at[11])
    bias_load = pltpu.make_async_copy(bias_hbm, bias, w_sem.at[12])
    for load in loads[:6]:
        load.start()
    dout_load.start()
    for load in loads[6:]:
        load.start()
    bias_load.start()

    barrier = pltpu.get_barrier_semaphore()

    def greet(device):
        pl.semaphore_signal(barrier, inc=1, device_id=device, device_id_type=MESH)

    for o in range(1, H):
        greet((s, wrap(h + o, H)))
    for o in range(1, side):
        greet((wrap(sx + o, side) * side + sy, h))
        greet((sx * side + wrap(sy + o, side), h))
    greet((wrap(s + 1, S), h))
    greet((wrap(s + S - 1, S), h))
    at_end = (z == planes - 1) & (c == 1)
    begins = (z == 1) | (z == 2)

    @pl.when(at_end)
    def _():
        for zo in (1, 2):
            for ch in range(2):
                greet((wrap(s + 1, S), 2 * zo + ch))

    @pl.when(begins)
    def _():
        greet((wrap(s + S - 1, S), H - 1))
        greet((wrap(s + S - 1, S), far_head))

    ends = (z == 1 + planes // 2) | (z == 2 + planes // 2)

    @pl.when(ends)
    def _():
        greet((wrap(s + 1, S), far_head))

    greeted = (
        H - 1 + 2 * (side - 1) + 2
        + jnp.where(at_end, 4, 0) + jnp.where(begins, 2, 0) + jnp.where(ends, 1, 0)
    )

    gain = gain_ref[...].astype(F32).reshape(1, D)
    loads[0].wait()
    x = act[...].astype(F32)
    centred = x - jnp.mean(x, axis=1, keepdims=True)
    inv = lax.rsqrt(jnp.mean(centred * centred, axis=1, keepdims=True) + EPS)
    xhat = centred * inv
    scaled[...] = xhat
    inverse[...] = jnp.broadcast_to(inv, inverse.shape)
    normed[...] = (xhat * gain).astype(BF16)

    def target(d):
        if d in (0, 1, 2, planes - 2, planes - 1):
            return d, starts[near] + 1 + 2 * ((near // 2 - d) % planes)
        return (d + planes // 2) % planes, starts[far] + 1 + 2 * ((far // 2 - d - planes // 2) % planes)

    def forward_copy(d, ch):
        up, place = target(d)
        head = 2 * wrap(z + d, planes) + ch
        return remote(
            send.at[head], recv.at[place + c], f_send.at[2 * d + ch], f_recv.at[place + c],
            (s, 2 * wrap(z + up, planes) + ch),
        )

    def own_copy(d):
        place = target(d)[1] + c
        head = 2 * wrap(z + d, planes) + c
        return pltpu.make_async_copy(send.at[head], recv.at[place], f_recv.at[place])

    def arrival(place):
        return pltpu.make_async_copy(recv.at[place], recv.at[place], f_recv.at[place])

    close = [(d, ch) for d in (0, 1, planes - 1, 4, 5, 3) for ch in range(2)]
    distant = [(d, ch) for d in (2, planes - 2) for ch in range(2)]
    sends = close + distant

    def send_some(which, half):
        for d, ch in which:
            head = 2 * wrap(z + d, planes) + ch
            now = True if half is None else head // half_heads == half
            if d in (0, planes // 2):
                now = now & (c != ch)
            if now is True:
                forward_copy(d, ch).start()
            else:
                @pl.when(now)
                def _(d=d, ch=ch):
                    forward_copy(d, ch).start()

    def by_head(product):
        return product.T.astype(BF16).reshape(half_heads, DH, PAIR)

    cross_bias = remote(
        bias_hbm.at[s], far_bias.at[sx, sy], c_send.at[0], c_recv.at[0], (s, far_head)
    )
    my_half = h // half_heads
    for turn in range(2):
        half = my_half if turn == 0 else 1 - my_half
        cols = mine if turn == 0 else rest
        heads = pl.ds(half * half_heads, half_heads)
        rows_in = normed[...]
        for i, (w, rows) in enumerate(((wq, q_rows), (wk, k_rows), (wv, v_rows))):
            loads[1 + 5 * turn + i].wait()
            send[heads, rows, :] = by_head(mm(rows_in, w[:, cols], ((1,), (0,))))
        for load in loads[4 + 5 * turn:6 + 5 * turn]:
            load.wait()
        if turn == 0:
            dout_load.wait()
        gate_in = by_head(mm(rows_in, wg[:, cols], ((1,), (0,))))
        mixed = mm(wo[cols, :], dout[...], ((1,), (1,))).astype(BF16)
        mixed = mixed.reshape(half_heads, DH, PAIR)
        gin[heads] = gate_in
        dmix[heads] = mixed
        gate = jax.nn.sigmoid(gate_in.astype(F32))
        send[heads, g_rows, :] = (mixed.astype(F32) * gate).astype(BF16)
        if turn == 0:
            pl.semaphore_wait(barrier, greeted)
            cross_bias.start()
            own_copy(0).start()
        else:
            own_copy(planes // 2).start()
        send_some(close, half)

    def key_start(run, ch):
        up = run // 2 + 1
        zo = wrap(z + up, planes)
        head = 2 * (zo if run == near else wrap(zo + planes // 2, planes)) + ch
        group = wrap(s + jnp.where(z == planes - 1, 1, 0), S)
        i = 0 if run == near else 1
        return remote(
            send.at[head, kv_rows, last_block], recv.at[starts[run], kv_rows, last_block],
            k_send.at[2 * i + ch], k_recv.at[i], (group, 2 * zo + ch),
        )

    gives_start = (c == 1) & ((z < planes - 1) | (s < S - 1))

    @pl.when(gives_start)
    def _():
        for ch in range(2):
            key_start(far, ch).start()

    send_some(distant, None)

    @pl.when(gives_start)
    def _():
        for ch in range(2):
            key_start(near, ch).start()

    crops = lengths_ref.shape[0]
    row = lax.broadcasted_iota(jnp.int32, (crops, PAIR), 0)
    lane = lax.broadcasted_iota(jnp.int32, (crops, PAIR), 1)
    low = jnp.zeros((crops, PAIR), jnp.int32)
    high = jnp.zeros((crops, PAIR), jnp.int32)
    total = jnp.int32(0)
    for crop in range(crops):
        low = jnp.where(row == crop, total, low)
        total = total + lengths_ref[crop]
        high = jnp.where(row == crop, total, high)
    for j in range(H + 1):
        pos = (s * H + j - 1) * PAIR + lane
        inside = (pos >= low) & (pos < high)
        hotq[j] = jnp.where(inside, 1.0, 0.0).astype(BF16)
        hotk[j] = jnp.where(inside, 0.0, UNSEEN).astype(BF16)

    def first_pair(run):
        return 2 * wrap(z - run // 2, planes)

    order_at = {near: 0, far: 4 * near}
    for run in (near, far):
        for i in range(2 * run):
            p = run + i // 2 if i % 2 == 0 else run - 1 - i // 2
            j = wrap(first_pair(run) + p, H)
            for b in range(2):
                order[order_at[run] + 2 * i + b] = tiles_ref[2 * j + b]

    def latest(run, tile, before):
        found = jnp.int32(-1)
        for slot in range(order_at[run], order_at[run] + 4 * run):
            found = jnp.where((order[slot] == tile) & (slot < before), slot, found)
        return found

    def clear(n, carry):
        chain[n] = jnp.zeros((BLOCK, PAIR), F32)
        return carry

    lax.fori_loop(0, 2 * H, clear, 0)

    edge_ids = {near: 0, far: 1}

    def has_start(run):
        return (s > 0) | (first_pair(run) != 0)

    def ends_group(run):
        return wrap(first_pair(run) + 2 * run - 1, H) == H - 1

    def has_end(run):
        return (s < S - 1) | jnp.logical_not(ends_group(run))

    def crosses(run):
        return (first_pair(run) != 0) & (first_pair(run) + 2 * run > H)

    for run in (near, far):
        @pl.when(jnp.logical_not(has_start(run)))
        def _(run=run):
            recv[starts[run]] = jnp.zeros((4 * DH, PAIR), BF16)

        @pl.when(crosses(run) & (s == 0))
        def _(run=run):
            recv[wraps[run]] = jnp.zeros((4 * DH, PAIR), BF16)

        @pl.when(jnp.logical_not(has_end(run)))
        def _(run=run):
            nxt[starts[run] + 2 * run + 1] = jnp.zeros((2 * DH, BLOCK), F32)

        @pl.when(crosses(run) & (s == S - 1))
        def _(run=run):
            nxt[nxt_wraps[run]] = jnp.zeros((2 * DH, BLOCK), F32)

    def key_wrap(run):
        at = starts[run] + 1 + wrap(H - 1 - first_pair(run), H)
        i = edge_ids[run]
        return remote(
            recv.at[at, kv_rows, last_block], recv.at[wraps[run], kv_rows, last_block],
            k_send.at[4 + i], k_recv.at[2 + i], (wrap(s + 1, S), h),
        )

    def grad_wrap(run):
        i = edge_ids[run]
        return remote(
            edge_out.at[2 + i], edge_in.at[2 + i], e_send.at[2 + i], e_recv.at[2 + i],
            (wrap(s + S - 1, S), h),
        )

    def grad_start(run):
        i = edge_ids[run]
        group = wrap(s - jnp.where(first_pair(run) == 0, 1, 0), S)
        return remote(
            edge_out.at[i], edge_in.at[1 - i], e_send.at[i], e_recv.at[1 - i], (group, far_head)
        )

    def edge_arrival(i):
        return pltpu.make_async_copy(edge_in.at[i], edge_in.at[i], e_recv.at[i])

    def key_arrival(place, i):
        part = recv.at[place, kv_rows, last_block]
        return pltpu.make_async_copy(part, part, k_recv.at[i])

    def back_copy(run, p):
        place = starts[run] + 1 + p
        return remote(
            res.at[place], got.at[heads_of[run]], b_send.at[place], b_recv.at[heads_of[run]],
            (s, wrap(first_pair(run) + p, H)),
        )

    def own_back(run):
        place = starts[run] + 1 + run - 1 + c
        return pltpu.make_async_copy(res.at[place], got.at[heads_of[run]], b_recv.at[heads_of[run]])

    def back_arrival(head):
        return pltpu.make_async_copy(got.at[head], got.at[head], b_recv.at[head])

    def finish(run, p, after):
        place = starts[run] + 1 + p
        later = nxt[after]
        sums = own[place]
        res[place, pl.ds(2 * DH, 2 * DH), pl.ds(0, BLOCK)] = sums[:, :BLOCK].astype(BF16)
        res[place, pl.ds(2 * DH, 2 * DH), last_block] = (sums[:, BLOCK:] + later).astype(BF16)
        mine_too = p == run - 1 + c

        @pl.when(mine_too)
        def _():
            own_back(run).start()

        @pl.when(jnp.logical_not(mine_too))
        def _():
            back_copy(run, p).start()

    def attend(tiles, place, before_place, j, b, slot, before):
        lanes = pl.ds(b * BLOCK, BLOCK)
        q = recv[place, q_rows, lanes]
        g = recv[place, g_rows, lanes]
        if b == 0:
            k = jnp.concatenate(
                [recv[before_place, k_rows, last_block], recv[place, k_rows, lanes]], axis=1
            )
            v = jnp.concatenate(
                [recv[before_place, v_rows, last_block], recv[place, v_rows, lanes]], axis=1
            )
            hot = jnp.concatenate([hotk[j, :, last_block], hotk[j + 1, :, lanes]], axis=1)
        else:
            k = recv[place, k_rows, :]
            v = recv[place, v_rows, :]
            hot = hotk[j + 1]
        q_all = jnp.concatenate([q, hotq[j + 1, :, lanes]], axis=0)
        k_all = jnp.concatenate([k, hot], axis=0)
        scores = mm(q_all, k_all, ((0,), (0,))) * scale + tiles(order[slot]).astype(F32)
        weights = jnp.exp(scores - jnp.max(scores, axis=1, keepdims=True))
        probs = weights * (1.0 / jnp.sum(weights, axis=1, keepdims=True))
        probs_low = probs.astype(BF16)
        d_probs = mm(g, v, ((0,), (0,)))
        weighted = probs * d_probs
        d_scores = weighted - probs * jnp.sum(weighted, axis=1, keepdims=True)
        d_low = d_scores.astype(BF16)
        res[place, pl.ds(0, DH), lanes] = mm(v, probs_low, ((1,), (1,))).astype(BF16)
        res[place, pl.ds(DH, DH), lanes] = (mm(k, d_low, ((1,), (1,))) * scale).astype(BF16)
        kept = jnp.where(before >= 0, chain[jnp.maximum(before, 0)], 0.0)
        chain[slot] = kept + d_scores
        d_k = mm(q, d_low, ((1,), (0,))) * scale
        d_v = mm(g, probs_low, ((1,), (0,)))
        return d_k, d_v

    def work(run, tiles, begin, end, beside):
        base = starts[run] + 1
        e = edge_ids[run]
        wraps_at = wrap(H - first_pair(run), H)

        def step(i, carry):
            up = lax.rem(i, 2) == 0
            p = jnp.where(up, run + i // 2, run - 1 - i // 2)
            j = wrap(first_pair(run) + p, H)
            arrived = jnp.where(up, p, p - 1)
            beside(i)

            @pl.when(arrived >= 0)
            def _():
                @pl.when(i > 0)
                def _():
                    arrival(base + arrived).wait()

                @pl.when(crosses(run) & (s < S - 1) & (arrived == wraps_at - 1))
                def _():
                    key_wrap(run).start()

            @pl.when((arrived < 0) & has_start(run))
            def _():
                key_arrival(starts[run], e).wait()

            inner = crosses(run) & (p == wraps_at)

            @pl.when(inner & (s > 0))
            def _():
                key_arrival(wraps[run], 2 + e).wait()

            place = base + p
            before_place = jnp.where(inner, wraps[run], place - 1)
            slot = order_at[run] + 2 * i
            first_k, first_v = attend(
                tiles, place, before_place, j, 0, slot, latest(run, order[slot], slot)
            )
            second_k, second_v = attend(
                tiles, place, before_place, j, 1, slot + 1,
                latest(run, order[slot + 1], slot + 1),
            )
            nxt[place, pl.ds(0, DH), :] = first_k[:, :BLOCK]
            nxt[place, pl.ds(DH, DH), :] = first_v[:, :BLOCK]
            own[place, pl.ds(0, DH), pl.ds(0, BLOCK)] = first_k[:, BLOCK:] + second_k[:, :BLOCK]
            own[place, pl.ds(DH, DH), pl.ds(0, BLOCK)] = first_v[:, BLOCK:] + second_v[:, :BLOCK]
            own[place, pl.ds(0, DH), last_block] = second_k[:, BLOCK:]
            own[place, pl.ds(DH, DH), last_block] = second_v[:, BLOCK:]

            @pl.when(inner & (s > 0))
            def _():
                edge_out[2 + e] = nxt[place].astype(BF16)
                grad_wrap(run).start()

            @pl.when((p == 0) & has_start(run))
            def _():
                edge_out[e] = nxt[place].astype(BF16)
                grad_start(run).start()

            f = jnp.where(up, p - 1, p)

            @pl.when((i > 0) & jnp.logical_not(crosses(run) & (f == wraps_at - 1)))
            def _():
                finish(run, f, starts[run] + 2 + f)

            return carry

        lax.fori_loop(begin, end, step, 0)

    def passed_over(run):
        e = edge_ids[run]

        @pl.when(crosses(run))
        def _():
            @pl.when(s < S - 1)
            def _():
                edge_arrival(2 + e).wait()
                nxt[nxt_wraps[run]] = edge_in[2 + e].astype(F32)

            finish(run, wrap(H - first_pair(run), H) - 1, nxt_wraps[run])

    def last_of(run):
        e = edge_ids[run]

        @pl.when(has_end(run))
        def _():
            edge_arrival(e).wait()
            nxt[starts[run] + 2 * run + 1] = edge_in[e].astype(F32)

        finish(run, jnp.int32(2 * run - 1), starts[run] + 2 * run + 1)

    def x_of(o):
        return (wrap(sx + o, side) * side + sy, h)

    def y_of(o):
        return (sx * side + wrap(sy + o, side), h)

    def gather_copies(ref, a, b):
        one, two = [], []
        for o in range(1, side):
            one.append(remote(
                ref.at[sx, sy, upper], ref.at[sx, sy, upper], a.at[0, o], b.at[0, o], x_of(o)
            ))
            one.append(remote(
                ref.at[sx, sy, lower], ref.at[sx, sy, lower], a.at[1, o], b.at[1, o], y_of(o)
            ))
            two.append(remote(
                ref.at[:, sy, upper], ref.at[:, sy, upper], a.at[2, o], b.at[2, o], y_of(o)
            ))
            two.append(remote(
                ref.at[sx, :, lower], ref.at[sx, :, lower], a.at[3, o], b.at[3, o], x_of(o)
            ))
        return one, two

    def local(ref, sem):
        return pltpu.make_async_copy(ref, ref, sem)

    def gather_arrivals(ref, b):
        one, two = [], []
        for o in range(1, side):
            fx, fy = wrap(sx - o, side), wrap(sy - o, side)
            one.append(local(ref.at[fx, sy, upper], b.at[0, o]))
            one.append(local(ref.at[sx, fy, lower], b.at[1, o]))
            two.append(local(ref.at[:, fy, upper], b.at[2, o]))
            two.append(local(ref.at[fx, :, lower], b.at[3, o]))
        return one, two

    bias_one, bias_two = gather_copies(far_bias, g_send, g_recv)
    bias_in_one, bias_in_two = gather_arrivals(far_bias, g_recv)

    def bias_steps(i):
        @pl.when(i == 1)
        def _():
            local(far_bias.at[sx, sy], c_recv.at[0]).wait()
            for copy in bias_one:
                copy.start()

        @pl.when(i == 4)
        def _():
            for copy in bias_in_one:
                copy.wait()
            for copy in bias_two:
                copy.start()

    def scatter_one(k):
        copies = []
        for o in range(1, side):
            copies.append(remote(
                parts.at[k, wrap(sx + o, side), :, upper], first_a.at[k, o - 1],
                r_send.at[k, 0, o], r_recv.at[k, 0, o], x_of(o),
            ))
            copies.append(remote(
                parts.at[k, :, wrap(sy + o, side), lower], first_b.at[k, o - 1],
                r_send.at[k, 1, o], r_recv.at[k, 1, o], y_of(o),
            ))
        return copies

    def scatter_two(k):
        copies = []
        for o in range(1, side):
            copies.append(remote(
                mid_a.at[k, wrap(sy + o, side)], second_a.at[k, o - 1],
                r_send.at[k, 2, o], r_recv.at[k, 2, o], y_of(o),
            ))
            copies.append(remote(
                mid_b.at[k, wrap(sx + o, side)], second_b.at[k, o - 1],
                r_send.at[k, 3, o], r_recv.at[k, 3, o], x_of(o),
            ))
        return copies

    def begin_sums(run):
        k = edge_ids[run]

        def part(t, carry):
            at = latest(run, t, 2 * H)
            parts[k, t // side, lax.rem(t, side)] = jnp.where(
                at >= 0, chain[jnp.maximum(at, 0)], 0.0
            ).astype(BF16)
            return carry

        lax.fori_loop(0, S, part, 0)
        for copy in scatter_one(k):
            copy.start()

    def middle_sums(run):
        k = edge_ids[run]
        for o in range(1, side):
            local(first_a.at[k, o - 1], r_recv.at[k, 0, o]).wait()
            local(first_b.at[k, o - 1], r_recv.at[k, 1, o]).wait()
        for i in range(side):
            a = parts[k, sx, i, upper].astype(F32)
            b = parts[k, i, sy, lower].astype(F32)
            for o in range(side - 1):
                a = a + first_a[k, o, i].astype(F32)
                b = b + first_b[k, o, i].astype(F32)
            mid_a[k, i] = a.astype(BF16)
            mid_b[k, i] = b.astype(BF16)
        for copy in scatter_two(k):
            copy.start()

    def end_sums(run):
        k = edge_ids[run]
        for o in range(1, side):
            local(second_a.at[k, o - 1], r_recv.at[k, 2, o]).wait()
            local(second_b.at[k, o - 1], r_recv.at[k, 3, o]).wait()
        a = mid_a[k, sy].astype(F32)
        b = mid_b[k, sx].astype(F32)
        for o in range(side - 1):
            a = a + second_a[k, o].astype(F32)
            b = b + second_b[k, o].astype(F32)
        return a, b

    own_copy(0).wait()
    arrival(starts[near] + 1 + near - c).wait()
    bias_load.wait()
    work(near, lambda t: bias[t], 0, near, bias_steps)

    own_copy(planes // 2).wait()
    arrival(starts[far] + 1 + far - c).wait()
    for copy in bias_in_two:
        copy.wait()
    work(far, lambda t: far_bias[t // side, lax.rem(t, side)], 0, 2 * far, lambda i: None)
    begin_sums(far)
    passed_over(far)

    def sum_steps(i):
        @pl.when(i == near + 2)
        def _():
            middle_sums(far)

    work(near, lambda t: bias[t], near, 2 * near, sum_steps)
    begin_sums(near)
    far_a, far_b = end_sums(far)
    crossed[0, upper] = far_a.astype(BF16)
    crossed[0, lower] = far_b.astype(BF16)
    cross_sum = remote(
        crossed.at[0], crossed.at[1], c_send.at[1], c_recv.at[1], (s, far_head)
    )
    cross_sum.start()
    passed_over(near)
    last_of(far)
    last_of(near)
    gate = jax.nn.sigmoid(gin[...].astype(F32))
    gated[...] = dmix[...].astype(F32) * gate * (1.0 - gate)
    middle_sums(near)
    own_a, own_b = end_sums(near)
    local(crossed.at[1], c_recv.at[1]).wait()
    dbias_ref[sx, sy, upper] = (own_a + crossed[1, upper].astype(F32)).astype(BF16)
    dbias_ref[sx, sy, lower] = (own_b + crossed[1, lower].astype(F32)).astype(BF16)
    out_one, out_two = gather_copies(dbias_ref, a_send, a_recv)
    in_one, in_two = gather_arrivals(dbias_ref, a_recv)
    for copy in out_one:
        copy.start()
    for copy in in_one:
        copy.wait()
    for copy in out_two:
        copy.start()

    for head in range(H):
        back_arrival(head).wait()
    attended = got[:, pl.ds(0, DH), :].astype(F32)
    got[:, pl.ds(0, DH), :] = (gated[...] * attended).astype(BF16)
    chunk = 256

    def product(m, carry):
        rows = pl.ds(pl.multiple_of(m * chunk, chunk), chunk)
        acc = jnp.zeros((chunk, PAIR), F32)
        for i, w in enumerate((wg, wq, wk, wv)):
            grads = got[:, pl.ds(i * DH, DH), :].reshape(D, PAIR)
            acc = acc + mm(w[rows, :], grads, ((1,), (0,)))
        dnorm[rows, :] = acc
        return carry

    lax.fori_loop(0, D // chunk, product, 0)
    for piece in range(2):
        rows = pl.ds(piece * BLOCK, BLOCK)
        g = dnorm[:, rows].T * gain
        xhat = scaled[rows, :]
        centre = jnp.mean(g, axis=1, keepdims=True)
        along = jnp.mean(g * xhat, axis=1, keepdims=True)
        dact_ref[rows, :] = (inverse[rows, :1] * (g - centre - xhat * along)).astype(BF16)

    for copy in in_two:
        copy.wait()

    for d, ch in sends:
        if d in (0, planes // 2):
            @pl.when(c != ch)
            def _(d=d, ch=ch):
                forward_copy(d, ch).wait_send()
        else:
            forward_copy(d, ch).wait_send()
    cross_bias.wait_send()
    cross_sum.wait_send()
    for copy in bias_one + bias_two + out_one + out_two:
        copy.wait_send()
    for k in range(2):
        for copy in scatter_one(k) + scatter_two(k):
            copy.wait_send()

    @pl.when(gives_start)
    def _():
        for run in (near, far):
            for ch in range(2):
                key_start(run, ch).wait_send()

    for run in (near, far):
        @pl.when(crosses(run) & (s < S - 1))
        def _(run=run):
            key_wrap(run).wait_send()

        @pl.when(crosses(run) & (s > 0))
        def _(run=run):
            grad_wrap(run).wait_send()

        @pl.when(has_start(run))
        def _(run=run):
            grad_start(run).wait_send()

        for p in range(2 * run):
            if p in (run - 1, run):
                @pl.when(p != run - 1 + c)
                def _(run=run, p=p):
                    back_copy(run, p).wait_send()
            else:
                back_copy(run, p).wait_send()


def shards(H, S, activations, ln_gain, w_query, w_key, w_value, w_gate, w_out, bias_tiles,
           crop_lengths, tile_index, d_out):
    rows, D = activations.shape
    DH = D // H
    tiles = bias_tiles.shape[0]
    crops = crop_lengths.shape[0]
    vmem = pl.BlockSpec(memory_space=pltpu.VMEM)
    smem = pl.BlockSpec(memory_space=pltpu.SMEM)
    hbm = pl.BlockSpec(memory_space=pl.ANY)
    dma = pltpu.SemaphoreType.DMA
    side = math.isqrt(S)
    slots = H + 2
    half = BLOCK // 2
    d_act, d_bias = pl.pallas_call(
        functools.partial(kernel, H, S, DH),
        out_shape=(
            jax.ShapeDtypeStruct((rows, D), BF16),
            jax.ShapeDtypeStruct((side, side, BLOCK, PAIR), BF16),
        ),
        in_specs=[hbm, vmem, hbm, hbm, hbm, hbm, hbm, hbm, hbm, smem, smem],
        out_specs=(vmem, vmem),
        scratch_shapes=[
            pltpu.VMEM((rows, D), BF16),
            pltpu.VMEM((rows, D), BF16),
            pltpu.VMEM((tiles, BLOCK, PAIR), BF16),
            pltpu.VMEM((side, side, BLOCK, PAIR), BF16),
            pltpu.SMEM((2 * H,), jnp.int32),
            *[pltpu.VMEM((D, D), BF16) for _ in range(5)],
            pltpu.VMEM((rows, D), BF16),
            pltpu.VMEM((rows, D), F32),
            pltpu.VMEM((rows, 128), F32),
            pltpu.VMEM((H, DH, PAIR), BF16),
            pltpu.VMEM((H, DH, PAIR), BF16),
            pltpu.VMEM((H, 4 * DH, PAIR), BF16),
            pltpu.VMEM((slots + 2, 4 * DH, PAIR), BF16),
            pltpu.VMEM((slots, 4 * DH, PAIR), BF16),
            pltpu.VMEM((H, 4 * DH, PAIR), BF16),
            pltpu.VMEM((slots, 2 * DH, PAIR), F32),
            pltpu.VMEM((slots + 3, 2 * DH, BLOCK), F32),
            pltpu.VMEM((2 * H, BLOCK, PAIR), F32),
            pltpu.VMEM((H + 1, crops, PAIR), BF16),
            pltpu.VMEM((H + 1, crops, PAIR), BF16),
            pltpu.VMEM((4, 2 * DH, BLOCK), BF16),
            pltpu.VMEM((4, 2 * DH, BLOCK), BF16),
            pltpu.VMEM((2, side, side, BLOCK, PAIR), BF16),
            pltpu.VMEM((2, side - 1, side, half, PAIR), BF16),
            pltpu.VMEM((2, side - 1, side, half, PAIR), BF16),
            pltpu.VMEM((2, side, half, PAIR), BF16),
            pltpu.VMEM((2, side, half, PAIR), BF16),
            pltpu.VMEM((2, side - 1, half, PAIR), BF16),
            pltpu.VMEM((2, side - 1, half, PAIR), BF16),
            pltpu.VMEM((2, BLOCK, PAIR), BF16),
            pltpu.VMEM((D, PAIR), F32),
            pltpu.VMEM((H, DH, PAIR), F32),
            dma((13,)),
            dma((H,)), dma((slots,)), dma((slots,)), dma((H,)),
            dma((6,)), dma((4,)), dma((4,)), dma((4,)), dma((2,)), dma((2,)),
            dma((4, side)), dma((4, side)), dma((2, 4, side)), dma((2, 4, side)),
            dma((4, side)), dma((4, side)),
        ],
        compiler_params=pltpu.CompilerParams(
            collective_id=0, has_side_effects=True, vmem_limit_bytes=60 * 2**20
        ),
    )(
        activations, ln_gain, d_out, w_query, w_key, w_value, w_gate, w_out,
        bias_tiles.reshape(tiles, BLOCK, PAIR), crop_lengths, tile_index,
    )
    return d_act, d_bias.astype(F32).reshape(tiles, 1, BLOCK, PAIR)


def solution(mesh):
    return jax.shard_map(
        functools.partial(shards, mesh.shape["head"], mesh.shape["seq"]),
        mesh=mesh,
        in_specs=(
            P(("seq", "head"), None),
            P(),
            P(),
            P(),
            P(),
            P(),
            P(),
            P(None, "head", None, None),
            P(),
            P("seq"),
            P(("seq", "head"), None),
        ),
        out_specs=(P(("seq", "head"), None), P(None, "head", None, None)),
        check_vma=False,
    )
```

time: 95.7 us -> 89.5 us (0.935)
  the two profiles are of different devices: /device:TPU:32 before, /device:TPU:8 now
where the time goes in v2:
time: 89.5 us; the launch traced here: 89.4 us
  Pallas kernels  85.1 us (95%)
  other arithmetic  2.82 us (3%)
    pallas_call x1, Pallas kernels, shards(): pl.pallas_call(functools.partial(kernel, H, S, DH), out_shape=(jax.ShapeD...  85.1 us
    unnamed x1, other arithmetic  2.82 us

profile of v2, /device:TPU:8, one launch (start us, length us, event | category | flops | bytes accessed | tf_op | source)
XLA Modules:
  0.0 89.4 jit_solution(15974994524265376048)
XLA Ops:
  0.6 85.1 %shard_map.122 = (bf16[256,768]{1,0:T(8,128)(2,1)}, bf16[4,4,128,256]{3,2,1,0:T(8,128)(2,1)}) custom-call(bf16[256,768]{1,0:T(8,128)(2,1)} %act_hbm.1, bf16[768]{0:T(1024)(128)(2,1)} %gain_ref.1, bf16[256,768]{1,0:T(8,128)(2,1)} %dout_hbm.1, bf16[768,768]{1,0:T(8,128)(2,1)} %wq_hbm.1, bf16[768,768]{1,0:T(8,128)(2,1)} %wk_hbm.1, bf16[768,768]{1,0:T(8,128)(2,1)} %wv_hbm.1, ...), custom_call_target="tpu_custom_call" | custom-call | tf_op jit(solution)/shard_map/pallas_call | solution.py:734
  85.8 0.0 copy-start
  85.8 2.8 %convert.2 = f32[16,1,128,256]{3,2,1,0:T(8,128)} convert(bf16[16,1,128,256]{3,2,1,0:T(8,128)(2,1)} %bitcast.7) | non-fusion elementwise | flops 524288 | bytes 3145728
  88.6 0.0 copy-done
  88.6 0.7 copy.15
Async XLA Ops:
  85.8 2.8 %copy-start = (bf16[256,768]{1,0:T(8,128)(2,1)S(1)}, bf16[256,768]{1,0:T(8,128)(2,1)}, u32[]{:S(2)}) copy-start(bf16[256,768]{1,0:T(8,128)(2,1)} %get-tuple-element.10) | copy-start | bytes 1179652

commit v3 on v2

--- a/solution.py
+++ b/solution.py
@@ -26,7 +26,7 @@
     act_hbm, gain_ref, dout_hbm, wq_hbm, wk_hbm, wv_hbm, wg_hbm, wo_hbm, bias_hbm,
     lengths_ref, tiles_ref,
     dact_ref, dbias_ref,
-    act, dout, bias, far_bias, order, wq, wk, wv, wg, wo, normed, scaled, inverse, gin, dmix,
+    act, dout, bias, tile, own_tile, near_bias, far_bias, order, wq, wk, wv, wg, wo, normed, scaled, inverse, gin, dmix,
     send, recv, res, got, own, nxt, chain, hotq, hotk, edge_out, edge_in,
     parts, first_a, first_b, mid_a, mid_b, second_a, second_b, crossed, dnorm, gated,
     w_sem, f_send, f_recv, b_send, b_recv, k_send, k_recv, e_send, e_recv, c_send, c_recv,
@@ -44,7 +44,9 @@
     q_rows, k_rows, v_rows, g_rows = (pl.ds(i * DH, DH) for i in range(4))
     kv_rows = pl.ds(DH, 2 * DH)
     last_block = pl.ds(BLOCK, BLOCK)
-    upper, lower = pl.ds(0, BLOCK // 2), pl.ds(BLOCK // 2, BLOCK // 2)
+    out_halves = pl.ds(0, BLOCK // 2), pl.ds(BLOCK // 2, BLOCK // 2)
+    halves = pl.ds(0, BLOCK), pl.ds(BLOCK, BLOCK)
+    upper, lower = halves
     near, far = 5, 3
     starts = {near: 0, far: 2 * near + 1}
     total_slots = 2 * near + 2 * far + 2
@@ -76,8 +78,10 @@
         )
     dout_load = pltpu.make_async_copy(dout_hbm, dout, w_sem.at[11])
     bias_load = pltpu.make_async_copy(bias_hbm, bias, w_sem.at[12])
+    tile_load = pltpu.make_async_copy(bias_hbm.at[s], tile, w_sem.at[13])
     for load in loads[:6]:
         load.start()
+    tile_load.start()
     dout_load.start()
     for load in loads[6:]:
         load.start()
@@ -172,8 +176,12 @@
         return product.T.astype(BF16).reshape(half_heads, DH, PAIR)
 
     cross_bias = remote(
-        bias_hbm.at[s], far_bias.at[sx, sy], c_send.at[0], c_recv.at[0], (s, far_head)
+        own_tile, far_bias.at[sx, sy], c_send.at[0], c_recv.at[0], (s, far_head)
     )
+    tile_load.wait()
+    own_tile[...] = tile[...].astype(F32).T.astype(BF16)
+    pl.semaphore_wait(barrier, greeted)
+    cross_bias.start()
     my_half = h // half_heads
     for turn in range(2):
         half = my_half if turn == 0 else 1 - my_half
@@ -195,8 +203,6 @@
         gate = jax.nn.sigmoid(gate_in.astype(F32))
         send[heads, g_rows, :] = (mixed.astype(F32) * gate).astype(BF16)
         if turn == 0:
-            pl.semaphore_wait(barrier, greeted)
-            cross_bias.start()
             own_copy(0).start()
         else:
             own_copy(planes // 2).start()
@@ -261,10 +267,17 @@
         return found
 
     def clear(n, carry):
-        chain[n] = jnp.zeros((BLOCK, PAIR), F32)
+        chain[n] = jnp.zeros((PAIR, BLOCK), F32)
         return carry
 
     lax.fori_loop(0, 2 * H, clear, 0)
+
+    def turn_tile(n, carry):
+        near_bias[n] = bias[n].astype(F32).T.astype(BF16)
+        return carry
+
+    bias_load.wait()
+    lax.fori_loop(0, bias.shape[0], turn_tile, 0)
 
     edge_ids = {near: 0, far: 1}
 
@@ -374,20 +387,19 @@
             hot = hotk[j + 1]
         q_all = jnp.concatenate([q, hotq[j + 1, :, lanes]], axis=0)
         k_all = jnp.concatenate([k, hot], axis=0)
-        scores = mm(q_all, k_all, ((0,), (0,))) * scale + tiles(order[slot]).astype(F32)
-        weights = jnp.exp(scores - jnp.max(scores, axis=1, keepdims=True))
-        probs = weights * (1.0 / jnp.sum(weights, axis=1, keepdims=True))
+        scores = mm(k_all, q_all, ((0,), (0,))) * scale + tiles(order[slot]).astype(F32)
+        weights = jnp.exp(scores - jnp.max(scores, axis=0, keepdims=True))
+        probs = weights * (1.0 / jnp.sum(weights, axis=0, keepdims=True))
         probs_low = probs.astype(BF16)
-        d_probs = mm(g, v, ((0,), (0,)))
-        weighted = probs * d_probs
-        d_scores = weighted - probs * jnp.sum(weighted, axis=1, keepdims=True)
+        d_probs = mm(v, g, ((0,), (0,)))
+        d_scores = probs * (d_probs - jnp.sum(probs * d_probs, axis=0, keepdims=True))
         d_low = d_scores.astype(BF16)
-        res[place, pl.ds(0, DH), lanes] = mm(v, probs_low, ((1,), (1,))).astype(BF16)
-        res[place, pl.ds(DH, DH), lanes] = (mm(k, d_low, ((1,), (1,))) * scale).astype(BF16)
+        res[place, pl.ds(0, DH), lanes] = mm(v, probs_low, ((1,), (0,))).astype(BF16)
+        res[place, pl.ds(DH, DH), lanes] = (mm(k, d_low, ((1,), (0,))) * scale).astype(BF16)
         kept = jnp.where(before >= 0, chain[jnp.maximum(before, 0)], 0.0)
         chain[slot] = kept + d_scores
-        d_k = mm(q, d_low, ((1,), (0,))) * scale
-        d_v = mm(g, probs_low, ((1,), (0,)))
+        d_k = mm(q, d_low, ((1,), (1,))) * scale
+        d_v = mm(g, probs_low, ((1,), (1,)))
         return d_k, d_v
 
     def work(run, tiles, begin, end, beside):
@@ -487,7 +499,8 @@
     def y_of(o):
         return (sx * side + wrap(sy + o, side), h)
 
-    def gather_copies(ref, a, b):
+    def gather_copies(ref, a, b, halves):
+        upper, lower = halves
         one, two = [], []
         for o in range(1, side):
             one.append(remote(
@@ -507,7 +520,8 @@
     def local(ref, sem):
         return pltpu.make_async_copy(ref, ref, sem)
 
-    def gather_arrivals(ref, b):
+    def gather_arrivals(ref, b, halves):
+        upper, lower = halves
         one, two = [], []
         for o in range(1, side):
             fx, fy = wrap(sx - o, side), wrap(sy - o, side)
@@ -517,17 +531,15 @@
             two.append(local(ref.at[fx, :, lower], b.at[3, o]))
         return one, two
 
-    bias_one, bias_two = gather_copies(far_bias, g_send, g_recv)
-    bias_in_one, bias_in_two = gather_arrivals(far_bias, g_recv)
+    bias_one, bias_two = gather_copies(far_bias, g_send, g_recv, halves)
+    bias_in_one, bias_in_two = gather_arrivals(far_bias, g_recv, halves)
+
+    local(far_bias.at[sx, sy], c_recv.at[0]).wait()
+    for copy in bias_one:
+        copy.start()
 
     def bias_steps(i):
         @pl.when(i == 1)
-        def _():
-            local(far_bias.at[sx, sy], c_recv.at[0]).wait()
-            for copy in bias_one:
-                copy.start()
-
-        @pl.when(i == 4)
         def _():
             for copy in bias_in_one:
                 copy.wait()
@@ -563,15 +575,19 @@
     def begin_sums(run):
         k = edge_ids[run]
 
-        def part(t, carry):
-            at = latest(run, t, 2 * H)
-            parts[k, t // side, lax.rem(t, side)] = jnp.where(
-                at >= 0, chain[jnp.maximum(at, 0)], 0.0
-            ).astype(BF16)
-            return carry
-
-        lax.fori_loop(0, S, part, 0)
-        for copy in scatter_one(k):
+        copies = scatter_one(k)
+        for o in (1, 2, 3, 0):
+            px = wrap(sx + o, side)
+
+            def part(py, carry, px=px):
+                at = latest(run, px * side + py, 2 * H)
+                parts[k, px, py] = jnp.where(at >= 0, chain[jnp.maximum(at, 0)], 0.0).astype(BF16)
+                return carry
+
+            lax.fori_loop(0, side, part, 0)
+            if o:
+                copies[2 * o - 2].start()
+        for copy in copies[1::2]:
             copy.start()
 
     def middle_sums(run):
@@ -604,8 +620,7 @@
 
     own_copy(0).wait()
     arrival(starts[near] + 1 + near - c).wait()
-    bias_load.wait()
-    work(near, lambda t: bias[t], 0, near, bias_steps)
+    work(near, lambda t: near_bias[t], 0, near, bias_steps)
 
     own_copy(planes // 2).wait()
     arrival(starts[far] + 1 + far - c).wait()
@@ -620,7 +635,7 @@
         def _():
             middle_sums(far)
 
-    work(near, lambda t: bias[t], near, 2 * near, sum_steps)
+    work(near, lambda t: near_bias[t], near, 2 * near, sum_steps)
     begin_sums(near)
     far_a, far_b = end_sums(far)
     crossed[0, upper] = far_a.astype(BF16)
@@ -637,10 +652,10 @@
     middle_sums(near)
     own_a, own_b = end_sums(near)
     local(crossed.at[1], c_recv.at[1]).wait()
-    dbias_ref[sx, sy, upper] = (own_a + crossed[1, upper].astype(F32)).astype(BF16)
-    dbias_ref[sx, sy, lower] = (own_b + crossed[1, lower].astype(F32)).astype(BF16)
-    out_one, out_two = gather_copies(dbias_ref, a_send, a_recv)
-    in_one, in_two = gather_arrivals(dbias_ref, a_recv)
+    sums = jnp.concatenate([own_a, own_b], axis=0) + crossed[1].astype(F32)
+    dbias_ref[sx, sy] = sums.T.astype(BF16)
+    out_one, out_two = gather_copies(dbias_ref, a_send, a_recv, out_halves)
+    in_one, in_two = gather_arrivals(dbias_ref, a_recv, out_halves)
     for copy in out_one:
         copy.start()
     for copy in in_one:
@@ -730,7 +745,6 @@
     dma = pltpu.SemaphoreType.DMA
     side = math.isqrt(S)
     slots = H + 2
-    half = BLOCK // 2
     d_act, d_bias = pl.pallas_call(
         functools.partial(kernel, H, S, DH),
         out_shape=(
@@ -743,7 +757,10 @@
             pltpu.VMEM((rows, D), BF16),
             pltpu.VMEM((rows, D), BF16),
             pltpu.VMEM((tiles, BLOCK, PAIR), BF16),
-            pltpu.VMEM((side, side, BLOCK, PAIR), BF16),
+            pltpu.VMEM((BLOCK, PAIR), BF16),
+            pltpu.VMEM((PAIR, BLOCK), BF16),
+            pltpu.VMEM((tiles, PAIR, BLOCK), BF16),
+            pltpu.VMEM((side, side, PAIR, BLOCK), BF16),
             pltpu.SMEM((2 * H,), jnp.int32),
             *[pltpu.VMEM((D, D), BF16) for _ in range(5)],
             pltpu.VMEM((rows, D), BF16),
@@ -757,22 +774,22 @@
             pltpu.VMEM((H, 4 * DH, PAIR), BF16),
             pltpu.VMEM((slots, 2 * DH, PAIR), F32),
             pltpu.VMEM((slots + 3, 2 * DH, BLOCK), F32),
-            pltpu.VMEM((2 * H, BLOCK, PAIR), F32),
+            pltpu.VMEM((2 * H, PAIR, BLOCK), F32),
             pltpu.VMEM((H + 1, crops, PAIR), BF16),
             pltpu.VMEM((H + 1, crops, PAIR), BF16),
             pltpu.VMEM((4, 2 * DH, BLOCK), BF16),
             pltpu.VMEM((4, 2 * DH, BLOCK), BF16),
-            pltpu.VMEM((2, side, side, BLOCK, PAIR), BF16),
-            pltpu.VMEM((2, side - 1, side, half, PAIR), BF16),
-            pltpu.VMEM((2, side - 1, side, half, PAIR), BF16),
-            pltpu.VMEM((2, side, half, PAIR), BF16),
-            pltpu.VMEM((2, side, half, PAIR), BF16),
-            pltpu.VMEM((2, side - 1, half, PAIR), BF16),
-            pltpu.VMEM((2, side - 1, half, PAIR), BF16),
-            pltpu.VMEM((2, BLOCK, PAIR), BF16),
+            pltpu.VMEM((2, side, side, PAIR, BLOCK), BF16),
+            pltpu.VMEM((2, side - 1, side, BLOCK, BLOCK), BF16),
+            pltpu.VMEM((2, side - 1, side, BLOCK, BLOCK), BF16),
+            pltpu.VMEM((2, side, BLOCK, BLOCK), BF16),
+            pltpu.VMEM((2, side, BLOCK, BLOCK), BF16),
+            pltpu.VMEM((2, side - 1, BLOCK, BLOCK), BF16),
+            pltpu.VMEM((2, side - 1, BLOCK, BLOCK), BF16),
+            pltpu.VMEM((2, PAIR, BLOCK), BF16),
             pltpu.VMEM((D, PAIR), F32),
             pltpu.VMEM((H, DH, PAIR), F32),
-            dma((13,)),
+            dma((14,)),
             dma((H,)), dma((slots,)), dma((slots,)), dma((H,)),
             dma((6,)), dma((4,)), dma((4,)), dma((4,)), dma((2,)), dma((2,)),
             dma((4, side)), dma((4, side)), dma((2, 4, side)), dma((2, 4, side)),

time: 89.5 us -> 81.8 us (0.914)
  Pallas kernels: 85.1 us -> 76.8 us
    pallas_call x1, Pallas kernels: 85.1 us -> 76.8 us  [shards(): pl.pallas_call(functools.partial(kernel, H, S, DH), out_shape=(jax.ShapeD...]
where the time goes in v3:
time: 81.8 us; the launch traced here: 81 us
  Pallas kernels  76.8 us (94%)
  other arithmetic  2.82 us (3%)
    pallas_call x1, Pallas kernels, shards(): pl.pallas_call(functools.partial(kernel, H, S, DH), out_shape=(jax.ShapeD...  76.8 us
    unnamed x1, other arithmetic  2.82 us

profile of v3, /device:TPU:8, one launch (start us, length us, event | category | flops | bytes accessed | tf_op | source)
XLA Modules:
  0.0 81.0 jit_solution(3468370716021152642)
XLA Ops:
  0.6 76.8 %shard_map.122 = (bf16[256,768]{1,0:T(8,128)(2,1)}, bf16[4,4,128,256]{3,2,1,0:T(8,128)(2,1)}) custom-call(bf16[256,768]{1,0:T(8,128)(2,1)} %act_hbm.1, bf16[768]{0:T(1024)(128)(2,1)} %gain_ref.1, bf16[256,768]{1,0:T(8,128)(2,1)} %dout_hbm.1, bf16[768,768]{1,0:T(8,128)(2,1)} %wq_hbm.1, bf16[768,768]{1,0:T(8,128)(2,1)} %wk_hbm.1, bf16[768,768]{1,0:T(8,128)(2,1)} %wv_hbm.1, ...), custom_call_target="tpu_custom_call" | custom-call | tf_op jit(solution)/shard_map/pallas_call | solution.py:748
  77.4 0.0 copy-start
  77.4 2.8 %convert.2 = f32[16,1,128,256]{3,2,1,0:T(8,128)} convert(bf16[16,1,128,256]{3,2,1,0:T(8,128)(2,1)} %bitcast.7) | non-fusion elementwise | flops 524288 | bytes 3145728
  80.3 0.0 copy-done
  80.3 0.7 copy.15
Async XLA Ops:
  77.4 2.8 %copy-start = (bf16[256,768]{1,0:T(8,128)(2,1)S(1)}, bf16[256,768]{1,0:T(8,128)(2,1)}, u32[]{:S(2)}) copy-start(bf16[256,768]{1,0:T(8,128)(2,1)} %get-tuple-element.10) | copy-start | bytes 1179652

commit v4 on v3

--- a/solution.py
+++ b/solution.py
@@ -173,7 +173,7 @@
                     forward_copy(d, ch).start()
 
     def by_head(product):
-        return product.T.astype(BF16).reshape(half_heads, DH, PAIR)
+        return product.astype(BF16).T.reshape(half_heads, DH, PAIR)
 
     cross_bias = remote(
         own_tile, far_bias.at[sx, sy], c_send.at[0], c_recv.at[0], (s, far_head)
@@ -266,14 +266,10 @@
             found = jnp.where((order[slot] == tile) & (slot < before), slot, found)
         return found
 
-    def clear(n, carry):
-        chain[n] = jnp.zeros((PAIR, BLOCK), F32)
-        return carry
-
-    lax.fori_loop(0, 2 * H, clear, 0)
+    chain[0] = jnp.zeros((PAIR, BLOCK), F32)
 
     def turn_tile(n, carry):
-        near_bias[n] = bias[n].astype(F32).T.astype(BF16)
+        near_bias[n] = bias[n].T
         return carry
 
     bias_load.wait()

time: 81.8 us -> 81.1 us (level)
  no operation moved by 1% of the time
where the time goes in v4:
time: 81.1 us; the launch traced here: 81 us
  Pallas kernels  76.8 us (95%)
  other arithmetic  2.82 us (3%)
    pallas_call x1, Pallas kernels, shards(): pl.pallas_call(functools.partial(kernel, H, S, DH), out_shape=(jax.ShapeD...  76.8 us
    unnamed x1, other arithmetic  2.82 us

profile of v4, /device:TPU:8, one launch (start us, length us, event | category | flops | bytes accessed | tf_op | source)
XLA Modules:
  0.0 81.0 jit_solution(8922697658744760075)
XLA Ops:
  0.6 76.8 %shard_map.122 = (bf16[256,768]{1,0:T(8,128)(2,1)}, bf16[4,4,128,256]{3,2,1,0:T(8,128)(2,1)}) custom-call(bf16[256,768]{1,0:T(8,128)(2,1)} %act_hbm.1, bf16[768]{0:T(1024)(128)(2,1)} %gain_ref.1, bf16[256,768]{1,0:T(8,128)(2,1)} %dout_hbm.1, bf16[768,768]{1,0:T(8,128)(2,1)} %wq_hbm.1, bf16[768,768]{1,0:T(8,128)(2,1)} %wk_hbm.1, bf16[768,768]{1,0:T(8,128)(2,1)} %wv_hbm.1, ...), custom_call_target="tpu_custom_call" | custom-call | tf_op jit(solution)/shard_map/pallas_call | solution.py:744
  77.4 0.0 copy-start
  77.4 2.8 %convert.2 = f32[16,1,128,256]{3,2,1,0:T(8,128)} convert(bf16[16,1,128,256]{3,2,1,0:T(8,128)(2,1)} %bitcast.7) | non-fusion elementwise | flops 524288 | bytes 3145728
  80.2 0.0 copy-done
  80.2 0.7 copy.15
Async XLA Ops:
  77.4 2.8 %copy-start = (bf16[256,768]{1,0:T(8,128)(2,1)S(1)}, bf16[256,768]{1,0:T(8,128)(2,1)}, u32[]{:S(2)}) copy-start(bf16[256,768]{1,0:T(8,128)(2,1)} %get-tuple-element.10) | copy-start | bytes 1179652
